TPU v7x, 512 devices: a whole 4x4x16 slice. The times are simulated.
512 devices in a mesh: shot: 2 (over core), tx: 8 (over z_hi, y), ty: 32 (over z_lo, x).
Axes of the slice: x: 4, y: 4, z: 16 (z_hi: 2, z_lo: 8; z = z_hi * 8 + z_lo), core: 2. Of those that a mesh axis runs over, the one named last changes fastest.
Arguments:
- forward_fields: float32 [2, 9, 128, 512, 128], P('shot', None, 'tx', 'ty'), may hold values from -6 to 6
- adjoint_fields: float32 [2, 9, 128, 512, 128], P('shot', None, 'tx', 'ty'), may hold values from -6 to 6
- lame_lambda: float32 [128, 512, 128], P('tx', 'ty'), may hold values from 1 to 4
- shear_modulus: float32 [128, 512, 128], P('tx', 'ty'), may hold values from 0.5 to 2
- density: float32 [128, 512, 128], P('tx', 'ty'), may hold values from 1 to 3
- source_cell: int32 [2], P('shot'), may hold values from 0 to 8388607
- source_amp: float32 [2], P('shot'), may hold values from 4 to 12
- receiver_cell: int32 [2, 256], P('shot'), may hold values from 0 to 8388607
- residual_amp: float32 [2, 256], P('shot'), may hold values from -16 to 16
Outputs:
- forward_next: float32 [2, 9, 128, 512, 128], P('shot', None, 'tx', 'ty')
- adjoint_next: float32 [2, 9, 128, 512, 128], P('shot', None, 'tx', 'ty')
- gradient: float32 [3, 128, 512, 128], P(None, 'tx', 'ty')
Inputs may be any that keep to these rules, and one draw needn't show every extreme that they name: `source_cell`: each value is a flat index x * 512 * 128 + y * 128 + z of a grid cell. `receiver_cell`: each value is a flat index x * 512 * 128 + y * 128 + z of a grid cell; receivers may share cells.
All inputs are finite; a program needn't handle non-finite values.
Results may differ from a plain program's by a relative error of at most 0.0001.
Values sent between devices are 32-bit elements; how exact they have to be, the bound alone decides.
A program may use at most 64 MiB of HBM per device.

v0:
```python
import jax
import jax.numpy as jnp
from jax import lax
from jax.sharding import PartitionSpec as P

near_coef = 9.0 / 8.0
far_coef = -1.0 / 24.0
time_step = 0.15


def extended(value, sides, width):
    for axis, dim in sides:
        peers, length = (lax.axis_size(axis), value.shape[dim])
        up = [(i, (i + 1) % peers) for i in range(peers - 1)]
        down = [(j, i) for i, j in up]
        last = lax.slice_in_dim(value, length - width, length, axis=dim)
        initial = lax.slice_in_dim(value, 0, width, axis=dim)
        before = lax.ppermute(last, axis, up)
        after = lax.ppermute(initial, axis, down)
        value = jnp.concatenate([before, value, after], axis=dim)
    return value


def shifted(padded, margin, rim_width, direction, offset):
    rank_count = padded.ndim
    sliced = padded
    for which in range(3):
        length = padded.shape[rank_count - 3 + which] - 2 * margin[which] + 2 * rim_width[which]
        begin_at = margin[which] - rim_width[which] + (offset if which == direction else 0)
        sliced = lax.slice_in_dim(sliced, begin_at, begin_at + length, axis=rank_count - 3 + which)
    return sliced


def depth_table(depth_cells, upward):
    source_row = lax.broadcasted_iota(jnp.int32, (depth_cells, depth_cells), 0)
    target_col = lax.broadcasted_iota(jnp.int32, (depth_cells, depth_cells), 1)
    gap = source_row - target_col
    if upward:
        table = near_coef * (
            (gap == 1).astype(jnp.float32) - (gap == 0).astype(jnp.float32)
        ) + far_coef * ((gap == 2).astype(jnp.float32) - (gap == -1).astype(jnp.float32))
    else:
        table = near_coef * (
            (gap == 0).astype(jnp.float32) - (gap == -1).astype(jnp.float32)
        ) + far_coef * ((gap == 1).astype(jnp.float32) - (gap == -2).astype(jnp.float32))
    return table


def derive(padded, margin, rim_width, direction, upward):
    if direction == 2:
        core = shifted(padded, margin, rim_width, 2, 0)
        return jnp.einsum(
            "...k,ki->...i",
            core,
            depth_table(core.shape[-1], upward),
            precision=lax.Precision.HIGHEST,
        )
    if upward:
        return near_coef * (
            shifted(padded, margin, rim_width, direction, 1)
            - shifted(padded, margin, rim_width, direction, 0)
        ) + far_coef * (
            shifted(padded, margin, rim_width, direction, 2)
            - shifted(padded, margin, rim_width, direction, -1)
        )
    return near_coef * (
        shifted(padded, margin, rim_width, direction, 0)
        - shifted(padded, margin, rim_width, direction, -1)
    ) + far_coef * (
        shifted(padded, margin, rim_width, direction, 1)
        - shifted(padded, margin, rim_width, direction, -2)
    )


def accelerate(stress_ext, buoyancy, margin, rim_width):
    comps = [stress_ext[..., which, :, :, :] for which in range(6)]
    accel_x = (
        derive(comps[0], margin, rim_width, 0, True)
        + derive(comps[3], margin, rim_width, 1, False)
        + derive(comps[4], margin, rim_width, 2, False)
    )
    accel_y = (
        derive(comps[3], margin, rim_width, 0, False)
        + derive(comps[1], margin, rim_width, 1, True)
        + derive(comps[5], margin, rim_width, 2, False)
    )
    accel_z = (
        derive(comps[4], margin, rim_width, 0, False)
        + derive(comps[5], margin, rim_width, 1, False)
        + derive(comps[2], margin, rim_width, 2, True)
    )
    return jnp.stack([accel_x, accel_y, accel_z], axis=-4) * buoyancy


def strain_rates(velocity_ext, margin):
    flat_rim = (0, 0, 0)
    comps = [velocity_ext[..., which, :, :, :] for which in range(3)]
    return jnp.stack(
        [
            derive(comps[0], margin, flat_rim, 0, False),
            derive(comps[1], margin, flat_rim, 1, False),
            derive(comps[2], margin, flat_rim, 2, False),
            derive(comps[0], margin, flat_rim, 1, True)
            + derive(comps[1], margin, flat_rim, 0, True),
            derive(comps[0], margin, flat_rim, 2, True)
            + derive(comps[2], margin, flat_rim, 0, True),
            derive(comps[1], margin, flat_rim, 2, True)
            + derive(comps[2], margin, flat_rim, 1, True),
        ],
        axis=-4,
    )


def new_stress(stress_now, strain, lame_lambda, shear_modulus):
    trace = strain[..., 0, :, :, :] + strain[..., 1, :, :, :] + strain[..., 2, :, :, :]
    normal = stress_now[..., :3, :, :, :] + time_step * (
        lame_lambda * trace[..., None, :, :, :] + 2.0 * shear_modulus * strain[..., :3, :, :, :]
    )
    shear = stress_now[..., 3:, :, :, :] + time_step * shear_modulus * strain[..., 3:, :, :, :]
    return jnp.concatenate([normal, shear], axis=-4)


def image_terms(strain_fwd, stress_adj, accel_fwd, velocity_adj):
    trace_fwd = (
        strain_fwd[..., 0, :, :, :] + strain_fwd[..., 1, :, :, :] + strain_fwd[..., 2, :, :, :]
    )
    trace_adj = (
        stress_adj[..., 0, :, :, :] + stress_adj[..., 1, :, :, :] + stress_adj[..., 2, :, :, :]
    )
    grad_lambda = -time_step * trace_fwd * trace_adj
    grad_shear = -time_step * jnp.sum(strain_fwd * stress_adj, axis=-4)
    grad_density = -time_step * jnp.sum(accel_fwd * velocity_adj, axis=-4)
    return jnp.stack([grad_lambda, grad_shear, grad_density], axis=-4)


def localize(cell_index, x_start, y_start, tile_x, tile_y, width_y, depth_cells):
    plane_size = width_y * depth_cells
    global_x = cell_index // plane_size
    remainder = cell_index % plane_size
    global_y = remainder // depth_cells
    global_z = remainder % depth_cells
    local_x = global_x - x_start
    local_y = global_y - y_start
    inside = (local_x >= 0) & (local_x < tile_x) & (local_y >= 0) & (local_y < tile_y)
    return jnp.where(
        inside, (local_x * tile_y + local_y) * depth_cells + global_z, tile_x * tile_y * depth_cells
    )


def inject(fields, where_cells, amounts):
    field_count, tile_x, tile_y, depth_cells = fields.shape
    column_count = tile_x * tile_y
    column = where_cells // depth_cells
    depth = where_cells % depth_cells
    column_hot = (column[:, None] == lax.broadcasted_iota(jnp.int32, (1, column_count), 1)).astype(
        jnp.float32
    )
    depth_hot = (depth[:, None] == lax.broadcasted_iota(jnp.int32, (1, depth_cells), 1)).astype(
        jnp.float32
    ) * amounts[:, None]
    added = jnp.dot(
        column_hot.T, depth_hot, precision=lax.Precision.HIGHEST, preferred_element_type=jnp.float32
    )
    added = added.reshape(1, tile_x, tile_y, depth_cells)
    return jnp.concatenate([fields[:3], fields[3:6] + added, fields[6:]], axis=0)


def body(
    forward_fields,
    adjoint_fields,
    lame_lambda,
    shear_modulus,
    density,
    source_cell,
    source_amp,
    receiver_cell,
    residual_amp,
):
    shot_count, field_count, tile_x, tile_y, depth_cells = forward_fields.shape
    width_y = tile_y * lax.axis_size("ty")
    x_start = lax.axis_index("tx") * tile_x
    y_start = lax.axis_index("ty") * tile_y
    source_local = localize(source_cell, x_start, y_start, tile_x, tile_y, width_y, depth_cells)
    receiver_local = localize(receiver_cell, x_start, y_start, tile_x, tile_y, width_y, depth_cells)
    forward = jax.vmap(inject)(forward_fields, source_local[:, None], source_amp[:, None])
    adjoint = jax.vmap(inject)(adjoint_fields, receiver_local, residual_amp)
    wavefields = jnp.concatenate([forward, adjoint], axis=0)
    buoyancy = 1.0 / density
    margin = (2, 2, 0)
    stress_ext = extended(wavefields[:, 3:], (("tx", 2), ("ty", 3)), 2)
    acceleration = accelerate(stress_ext, buoyancy, margin, (0, 0, 0))
    velocity = wavefields[:, :3] + time_step * acceleration
    velocity_ext = extended(velocity, (("tx", 2), ("ty", 3)), 2)
    strain = strain_rates(velocity_ext, margin)
    stress = new_stress(wavefields[:, 3:], strain, lame_lambda, shear_modulus)
    local_terms = jnp.sum(
        image_terms(
            strain[:shot_count],
            stress[shot_count:],
            acceleration[:shot_count],
            velocity[shot_count:],
        ),
        axis=0,
    )
    gradient = lax.psum(local_terms, "shot")
    stepped = jnp.concatenate([velocity, stress], axis=1)
    return (stepped[:shot_count], stepped[shot_count:], gradient)


def solution(mesh):
    return jax.shard_map(
        body,
        mesh=mesh,
        in_specs=(
            P("shot", None, "tx", "ty", None),
            P("shot", None, "tx", "ty", None),
            P("tx", "ty", None),
            P("tx", "ty", None),
            P("tx", "ty", None),
            P("shot"),
            P("shot"),
            P("shot", None),
            P("shot", None),
        ),
        out_specs=(
            P("shot", None, "tx", "ty", None),
            P("shot", None, "tx", "ty", None),
            P(None, "tx", "ty", None),
        ),
        check_vma=False,
    )
```

profile of v0, /device:TPU:1, one launch (start us, length us, event | category | flops | bytes accessed | tf_op | source)
XLA Modules:
  0.0 155.1 jit_solution(6553573474216581453)
XLA Ops:
  8.6 0.7 and_select_fusion
  9.6 1.1 fusion.53
  10.6 1.8 %fusion.168 = (f32[1,3,16,16,128]{4,3,2,1,0:T(8,128)S(1)}, f32[1,3,16,16,128]{4,3,2,1,0:T(8,128)S(1)}, f32[1,3,16,16,128]{4,3,2,1,0:T(8,128)S(1)}, f32[1,3,16,16...) fusion(f32[1,9,16,16,128]{4,3,2,1,0:T(8,128)} %param.9, ...), kind=kLoop, calls=%fused_computation.264 | loop fusion | flops 196608 | bytes 4980736 | tf_op jit(solution)/shard_map/vmap()/slice | solution.py:165
  12.5 4.0 %collective-permute-start = (f32[2,6,2,16,128]{4,3,2,1,0:T(8,128)S(1)}, f32[2,6,2,16,128]{4,3,2,1,0:T(8,128)S(1)}, u32[]{:S(2)}, u32[]{:S(2)}) collective-permute-start(f32[2,6,2,16,128]{4,3,2,1,0:T(8,128)S(1)} %get-tuple-element.25), channel_id=1, source_target_pairs={{0,32},{32,64},{64,96},{96,128},{128,160},{160,192},{192,224},{1,3... | collective-permute-start | bytes 589832 | tf_op jit(solution)/shard_map/ppermute | solution.py:18
  16.5 1.3 collective-permute-start.1
  18.1 1.0 collective-permute-done
  19.1 3.8 %collective-permute-done.1 = f32[2,6,2,16,128]{4,3,2,1,0:T(8,128)S(1)} collective-permute-done((f32[2,6,2,16,128]{4,3,2,1,0:T(8,128)S(1)}, f32[2,6,2,16,128]{4,3,2,1,0:T(8,128)S(1)}, u32[]{:S(2)}, u32[]{:S(2)}) %collective-permute-start.1) | collective-permute-done | bytes 196640 | tf_op jit(solution)/shard_map/ppermute | solution.py:19
  23.1 4.1 %collective-permute-start.2 = (f32[2,6,20,2,128]{4,3,2,1,0:T(2,128)S(1)}, f32[2,6,20,2,128]{4,3,2,1,0:T(2,128)S(1)}, u32[]{:S(2)}, u32[]{:S(2)}) collective-permute-start(f32[2,6,20,2,128]{4,3,2,1,0:T(2,128)S(1)} %get-tuple-element.27), channel_id=1, source_target_pairs={{0,1},{1,2},{2,3},{3,4},{4,5},{5,6},{6,7},{7,8},{8,9},{9,10},{10,1... | collective-permute-start | bytes 737288 | tf_op jit(solution)/shard_map/ppermute | solution.py:18
  27.2 1.3 collective-permute-start.3
  28.5 1.7 %collective-permute-done.2 = f32[2,6,20,2,128]{4,3,2,1,0:T(2,128)S(1)} collective-permute-done((f32[2,6,20,2,128]{4,3,2,1,0:T(2,128)S(1)}, f32[2,6,20,2,128]{4,3,2,1,0:T(2,128)S(1)}, u32[]{:S(2)}, u32[]{:S(2)}) %collective-permute-start.2) | collective-permute-done | bytes 245792 | tf_op jit(solution)/shard_map/ppermute | solution.py:18
  30.3 3.8 %collective-permute-done.3 = f32[2,6,20,2,128]{4,3,2,1,0:T(2,128)S(1)} collective-permute-done((f32[2,6,20,2,128]{4,3,2,1,0:T(2,128)S(1)}, f32[2,6,20,2,128]{4,3,2,1,0:T(2,128)S(1)}, u32[]{:S(2)}, u32[]{:S(2)}) %collective-permute-start.3) | collective-permute-done | bytes 245792 | tf_op jit(solution)/shard_map/ppermute | solution.py:19
  34.1 0.4 pad_maximum_fusion
  34.8 0.5 fusion.4
  35.2 0.5 fusion.2
  35.7 0.5 fusion.3
  36.4 3.2 %collective-permute-start.4 = (f32[2,3,2,16,128]{4,3,2,0,1:T(8,128)S(1)}, f32[2,3,2,16,128]{4,3,2,0,1:T(8,128)S(1)}, u32[]{:S(2)}, u32[]{:S(2)}) collective-permute-start(f32[2,3,2,16,128]{4,3,2,0,1:T(8,128)S(1)} %get-tuple-element.40), channel_id=1, source_target_pairs={{0,32},{32,64},{64,96},{96,128},{128,160},{160,192},{192,224},{1,3... | collective-permute-start | bytes 294920 | tf_op jit(solution)/shard_map/ppermute | solution.py:18
  39.6 1.3 collective-permute-start.5
  41.0 0.3 collective-permute-done.4
  41.2 15.9 %collective-permute-done.5 = f32[2,3,2,16,128]{4,3,2,0,1:T(8,128)S(1)} collective-permute-done((f32[2,3,2,16,128]{4,3,2,0,1:T(8,128)S(1)}, f32[2,3,2,16,128]{4,3,2,0,1:T(8,128)S(1)}, u32[]{:S(2)}, u32[]{:S(2)}) %collective-permute-start.5) | collective-permute-done | bytes 98336 | tf_op jit(solution)/shard_map/ppermute | solution.py:19
  57.3 3.1 %collective-permute-start.6 = (f32[2,3,20,2,128]{4,3,2,0,1:T(2,128)S(1)}, f32[2,3,20,2,128]{4,3,2,0,1:T(2,128)S(1)}, u32[]{:S(2)}, u32[]{:S(2)}) collective-permute-start(f32[2,3,20,2,128]{4,3,2,0,1:T(2,128)S(1)} %get-tuple-element.38), channel_id=1, source_target_pairs={{0,1},{1,2},{2,3},{3,4},{4,5},{5,6},{6,7},{7,8},{8,9},{9,10},{10,1... | collective-permute-start | bytes 368648 | tf_op jit(solution)/shard_map/ppermute | solution.py:18
  60.4 1.3 collective-permute-start.7
  61.7 0.5 collective-permute-done.6
  62.2 3.8 %collective-permute-done.7 = f32[2,3,20,2,128]{4,3,2,0,1:T(2,128)S(1)} collective-permute-done((f32[2,3,20,2,128]{4,3,2,0,1:T(2,128)S(1)}, f32[2,3,20,2,128]{4,3,2,0,1:T(2,128)S(1)}, u32[]{:S(2)}, u32[]{:S(2)}) %collective-permute-start.7) | collective-permute-done | bytes 122912 | tf_op jit(solution)/shard_map/ppermute | solution.py:19
  66.0 0.2 pad_maximum_fusion.2
  66.5 0.4 bitcast_dynamic-update-slice_fusion
  66.9 0.4 copy-done.1
  67.8 0.4 constant_dynamic-update-slice_fusion.1
  68.2 0.4 constant_dynamic-update-slice_fusion
  68.9 0.8 maximum_bitcast_fusion
  69.9 1.6 %slice_bitcast_fusion = (f32[1,9,16,16,128]{4,3,2,1,0:T(8,128)}, f32[1,9,16,16,128]{4,3,2,1,0:T(8,128)}) fusion(f32[2,9,16,16,128]{4,3,2,0,1:T(8,128)S(1)} %pad_maximum_fusion.1), kind=kLoop, calls=%fused_computation.4 | loop fusion | bytes 4718592
  71.4 75.1 %all-reduce.2.cloned.1.call-done = f32[3,16,16,128]{3,2,1,0:T(8,128)} async-done(((f32[3,16,16,128]{3,2,1,0:T(8,128)}), f32[3,16,16,128]{3,2,1,0:T(8,128)}) %all-reduce.2.cloned.1.call-update) | async-done | bytes 393232 | tf_op jit(solution)/shard_map/psum | solution.py:205
  146.5 1.8 %copy.46 = f32[3,16,16,128]{3,2,1,0:T(8,128)} copy(f32[3,16,16,128]{3,2,1,0:T(8,128)} %all-reduce.2.cloned.1.call-done) | data formatting | bytes 786432
  (37 shorter events, 2.5 us)
Async XLA Ops:
  7.2 139.3 %all-reduce.2.cloned.1.call-start = ((), (), s32[]{:S(2)}) async-start(), calls=%async_computation | async-start | bytes 786432 | tf_op jit(solution)/shard_map/psum | solution.py:205
  12.5 6.6 %collective-permute-start = (f32[2,6,2,16,128]{4,3,2,1,0:T(8,128)S(1)}, f32[2,6,2,16,128]{4,3,2,1,0:T(8,128)S(1)}, u32[]{:S(2)}, u32[]{:S(2)}) collective-permute-start(f32[2,6,2,16,128]{4,3,2,1,0:T(8,128)S(1)} %get-tuple-element.25), channel_id=1, source_target_pairs={{0,32},{32,64},{64,96},{96,128},{128,160},{160,192},{192,224},{1,3... | collective-permute-start | bytes 589832 | tf_op jit(solution)/shard_map/ppermute | solution.py:18
  16.5 6.4 %collective-permute-start.1 = (f32[2,6,2,16,128]{4,3,2,1,0:T(8,128)S(1)}, f32[2,6,2,16,128]{4,3,2,1,0:T(8,128)S(1)}, u32[]{:S(2)}, u32[]{:S(2)}) collective-permute-start(f32[2,6,2,16,128]{4,3,2,1,0:T(8,128)S(1)} %get-tuple-element.26), channel_id=1, source_target_pairs={{32,0},{64,32},{96,64},{128,96},{160,128},{192,160},{224,192},{33,... | collective-permute-start | bytes 589832 | tf_op jit(solution)/shard_map/ppermute | solution.py:19
  18.1 10.4 %copy-start.2 = (f32[16,16,128]{2,1,0:T(8,128)S(1)}, f32[16,16,128]{2,1,0:T(8,128)}, u32[]{:S(2)}) copy-start(f32[16,16,128]{2,1,0:T(8,128)} %param.13) | copy-start | bytes 393220
  18.1 10.4 %copy-start = (f32[16,16,128]{2,1,0:T(8,128)S(1)}, f32[16,16,128]{2,1,0:T(8,128)}, u32[]{:S(2)}) copy-start(f32[16,16,128]{2,1,0:T(8,128)} %param.12) | copy-start | bytes 393220
  23.1 7.2 %collective-permute-start.2 = (f32[2,6,20,2,128]{4,3,2,1,0:T(2,128)S(1)}, f32[2,6,20,2,128]{4,3,2,1,0:T(2,128)S(1)}, u32[]{:S(2)}, u32[]{:S(2)}) collective-permute-start(f32[2,6,20,2,128]{4,3,2,1,0:T(2,128)S(1)} %get-tuple-element.27), channel_id=1, source_target_pairs={{0,1},{1,2},{2,3},{3,4},{4,5},{5,6},{6,7},{7,8},{8,9},{9,10},{10,1... | collective-permute-start | bytes 737288 | tf_op jit(solution)/shard_map/ppermute | solution.py:18
  27.2 6.9 %collective-permute-start.3 = (f32[2,6,20,2,128]{4,3,2,1,0:T(2,128)S(1)}, f32[2,6,20,2,128]{4,3,2,1,0:T(2,128)S(1)}, u32[]{:S(2)}, u32[]{:S(2)}) collective-permute-start(f32[2,6,20,2,128]{4,3,2,1,0:T(2,128)S(1)} %get-tuple-element.28), channel_id=1, source_target_pairs={{1,0},{2,1},{3,2},{4,3},{5,4},{6,5},{7,6},{8,7},{9,8},{10,9},{11,1... | collective-permute-start | bytes 737288 | tf_op jit(solution)/shard_map/ppermute | solution.py:19
  36.4 4.8 %collective-permute-start.4 = (f32[2,3,2,16,128]{4,3,2,0,1:T(8,128)S(1)}, f32[2,3,2,16,128]{4,3,2,0,1:T(8,128)S(1)}, u32[]{:S(2)}, u32[]{:S(2)}) collective-permute-start(f32[2,3,2,16,128]{4,3,2,0,1:T(8,128)S(1)} %get-tuple-element.40), channel_id=1, source_target_pairs={{0,32},{32,64},{64,96},{96,128},{128,160},{160,192},{192,224},{1,3... | collective-permute-start | bytes 294920 | tf_op jit(solution)/shard_map/ppermute | solution.py:18
  39.6 17.5 %collective-permute-start.5 = (f32[2,3,2,16,128]{4,3,2,0,1:T(8,128)S(1)}, f32[2,3,2,16,128]{4,3,2,0,1:T(8,128)S(1)}, u32[]{:S(2)}, u32[]{:S(2)}) collective-permute-start(f32[2,3,2,16,128]{4,3,2,0,1:T(8,128)S(1)} %get-tuple-element.41), channel_id=1, source_target_pairs={{32,0},{64,32},{96,64},{128,96},{160,128},{192,160},{224,192},{33,... | collective-permute-start | bytes 294920 | tf_op jit(solution)/shard_map/ppermute | solution.py:19
  57.3 5.0 %collective-permute-start.6 = (f32[2,3,20,2,128]{4,3,2,0,1:T(2,128)S(1)}, f32[2,3,20,2,128]{4,3,2,0,1:T(2,128)S(1)}, u32[]{:S(2)}, u32[]{:S(2)}) collective-permute-start(f32[2,3,20,2,128]{4,3,2,0,1:T(2,128)S(1)} %get-tuple-element.38), channel_id=1, source_target_pairs={{0,1},{1,2},{2,3},{3,4},{4,5},{5,6},{6,7},{7,8},{8,9},{9,10},{10,1... | collective-permute-start | bytes 368648 | tf_op jit(solution)/shard_map/ppermute | solution.py:18
  60.4 5.6 %collective-permute-start.7 = (f32[2,3,20,2,128]{4,3,2,0,1:T(2,128)S(1)}, f32[2,3,20,2,128]{4,3,2,0,1:T(2,128)S(1)}, u32[]{:S(2)}, u32[]{:S(2)}) collective-permute-start(f32[2,3,20,2,128]{4,3,2,0,1:T(2,128)S(1)} %get-tuple-element.39), channel_id=1, source_target_pairs={{1,0},{2,1},{3,2},{4,3},{5,4},{6,5},{7,6},{8,7},{9,8},{10,9},{11,1... | collective-permute-start | bytes 368648 | tf_op jit(solution)/shard_map/ppermute | solution.py:19
  66.4 0.9 copy-start.1
Sparse Core Ops, SparseCore 0:
  69.8 76.6 all-reduce.1
where the time goes:
time: 156 us; the launch traced here: 155 us
  waiting for transfers between devices  106 us (68%)
  starting transfers between devices  19.6 us (13%)
  between operations  15.8 us (10%)
  other arithmetic  5.89 us (4%)
  local copies, waits for them, and re-layouts  4.22 us (3%)
  matrix products  3.63 us (2%)
    psum x1, waiting for transfers between devices, body(): gradient = lax.psum(local_terms, 'shot')  75.1 us
    ppermute x4, waiting for transfers between devices, extended(): after = lax.ppermute(initial, axis, down)  27.4 us
    ppermute x4, starting transfers between devices, extended(): before = lax.ppermute(last, axis, up)  14.4 us
    ppermute x4, starting transfers between devices, extended(): after = lax.ppermute(initial, axis, down)  5.17 us
    unnamed x8, local copies, waits for them, and re-layouts  3.73 us
    ppermute x4, waiting for transfers between devices, extended(): before = lax.ppermute(last, axis, up)  3.5 us
  transfers between devices with their start and end apart: 9, of which 9 were waited for; matrix products, arithmetic and copies ran while one was open for 1% of the time, Pallas kernels for 0%

commit v1 on v0

v1 whole, which is shorter than its diff:
```python
import functools

import jax
import jax.numpy as jnp
from jax import lax
from jax.experimental import pallas as pl
from jax.experimental.pallas import tpu as pltpu
from jax.sharding import PartitionSpec as P

C1 = 9.0 / 8.0
C2 = -1.0 / 24.0
DT = 0.15
MESH = pl.DeviceIdType.MESH
F32 = jnp.float32
CHUNK = 4
XX, YY, ZZ, XY, XZ, YZ = range(6)


def step_kernel(
    fwd, adj, lam_h, mu_h, den_h, scell_h, samp_h, rcell_h, ramp_h,
    f_out, a_out, g_out,
    ST, VE, VO, AC, BU, LM, MU, ADD, rcell, ramp, scell, samp,
    ysend, yrecv, bysend, byrecv, y2sb, y2sa, y2rb, y2ra,
    xs_send, xv_send, xs_recv, xv_recv, rel, GL, GR,
    in_sem, y_ss, y_rs, x_ss, x_rs, rel_ss, rel_rs, g_ss, g_rs,
):
    s, tx, ty = lax.axis_index("shot"), lax.axis_index("tx"), lax.axis_index("ty")
    last = lax.axis_size("ty") - 1
    partner = (1 - s, tx, ty)

    has_l, has_r = tx > 0, tx < 7
    near_l, near_r = (tx > 0) & (tx != 4), (tx < 7) & (tx != 3)
    lower, upper = ty > 0, ty < last
    is3, is4 = tx == 3, tx == 4
    low_relay, high_relay = tx < 3, tx > 4

    bar = pltpu.get_barrier_semaphore()

    def greet(cond, dev):
        @pl.when(cond)
        def _():
            pl.semaphore_signal(bar, inc=1, device_id=dev, device_id_type=MESH)

    for j in range(3):
        greet(is3, (s, 5 + j, ty))
        greet(is4, (s, j, ty))
    greet(lower, (s, tx, ty - 1))
    greet(upper, (s, tx, ty + 1))
    greet(near_l, (s, tx - 1, ty))
    greet(near_r, (s, tx + 1, ty))
    greet(tx < 2, (s, 3, ty))
    greet(tx > 5, (s, 4, ty))
    pl.semaphore_signal(bar, inc=1, device_id=partner, device_id_type=MESH)

    loads = [
        (fwd.at[0, pl.ds(3, 6)], ST.at[0, :, pl.ds(2, 16), pl.ds(8, 16)]),
        (adj.at[0, pl.ds(3, 6)], ST.at[1, :, pl.ds(2, 16), pl.ds(8, 16)]),
        (rcell_h, rcell),
        (ramp_h, ramp),
        (scell_h, scell),
        (samp_h, samp),
        (den_h, BU.at[pl.ds(2, 16), pl.ds(8, 16)]),
        (fwd.at[0, pl.ds(0, 3)], VO.at[0]),
        (adj.at[0, pl.ds(0, 3)], VO.at[1]),
        (lam_h, LM),
        (mu_h, MU),
    ]
    copies = [pltpu.make_async_copy(a, b, in_sem.at[i]) for i, (a, b) in enumerate(loads)]
    for c in copies:
        c.start()

    def clear(cond, ref, idx):
        @pl.when(cond)
        def _():
            ref[idx] = jnp.zeros(ref.at[idx].shape, F32)

    for w in range(2):
        for c in (XX, XY, XZ):
            for lo in (0, 18):
                ST[w, c, lo:lo + 2, 8:24, :] = jnp.zeros((2, 16, 128), F32)
    for side, gone in ((0, ty == 0), (1, ty == last)):
        clear(gone, yrecv, side)
        clear(gone, byrecv, side)
    clear(ty == 0, y2rb, slice(None))
    clear(ty == last, y2ra, slice(None))
    for side, gone in ((0, tx == 0), (1, tx == 7)):
        clear(gone, xs_recv, side)
        clear(gone, xv_recv, side)
    xs_send[1, 10:12] = jnp.zeros((2, 16, 128), F32)
    xv_send[0, 8:10] = jnp.zeros((2, 16, 128), F32)
    for side in range(2):
        for w in range(2):
            xv_send[side, 10 + w] = jnp.zeros((16, 128), F32)
    ysend[0, :, 8:16, :] = jnp.zeros((16, 8, 128), F32)
    y2sa[:, 8:16, :] = jnp.zeros((16, 8, 128), F32)

    for c in copies[2:6]:
        c.wait()

    def place(cell):
        lx = (cell >> 16) - tx * 16
        ly = ((cell >> 7) & 511) - ty * 16
        inside = (lx >= 0) & (lx < 16) & (ly >= 0) & (ly < 16)
        return jnp.where(inside, lx * 16 + ly, -1), cell & 127

    column, depth = place(rcell[...])
    hot = (lax.broadcasted_iota(jnp.int32, (256, 256), 0) == column).astype(jnp.bfloat16)
    amount = jnp.where(lax.broadcasted_iota(jnp.int32, (128, 256), 0) == depth, ramp[...], 0.0)
    high = amount.astype(jnp.bfloat16)
    rest = amount - high.astype(F32)
    mid = rest.astype(jnp.bfloat16)
    low = (rest - mid.astype(F32)).astype(jnp.bfloat16)
    nt = (((1,), (1,)), ((), ()))
    added = sum(
        lax.dot_general(hot, part, nt, preferred_element_type=F32) for part in (low, mid, high)
    )
    ADD[...] = added.reshape(16, 16, 128)
    scol, sdep = place(scell[0])
    ssum = samp[0]
    copies[0].wait()
    copies[1].wait()

    def inject_rows(i, carry):
        shape = (2, 16, 128)
        col = (lax.broadcasted_iota(jnp.int32, shape, 0) + 2 * i) * 16 + lax.broadcasted_iota(jnp.int32, shape, 1)
        dep = lax.broadcasted_iota(jnp.int32, shape, 2)
        hit = (col == scol) & (dep == sdep)
        src = jnp.where(hit, ssum, 0.0)
        rows = pl.ds(2 + 2 * i, 2)
        for c in range(3):
            ST[0, c, rows, 8:24, :] = ST[0, c, rows, 8:24, :] + src
            ST[1, c, rows, 8:24, :] = ST[1, c, rows, 8:24, :] + ADD[pl.ds(2 * i, 2)]
        return carry

    lax.fori_loop(0, 8, inject_rows, 0)
    copies[6].wait()
    BU[2:18, 8:24, :] = DT / BU[2:18, 8:24, :]

    for w in range(2):
        layers = [(XX, 15), (XY, 14), (XY, 15), (XZ, 14), (XZ, 15)]
        for i, (c, x) in enumerate(layers):
            xs_send[0, 5 * w + i] = ST[w, c, 2 + x, 8:24, :]
        layers = [(XX, 0), (XX, 1), (XY, 0), (XZ, 0)]
        for i, (c, x) in enumerate(layers):
            xs_send[1, 4 * w + i] = ST[w, c, 2 + x, 8:24, :]
    for i in range(2):
        xs_send[0, 10 + i] = BU[16 + i, 8:24, :]
        xs_send[1, 8 + i] = BU[2 + i, 8:24, :]
    for w in range(2):
        rows = [(XY, 14, 2), (YZ, 14, 2), (YY, 15, 1), (XX, 15, 1), (XZ, 15, 1)]
        k = 7 * w
        for c, y, n in rows:
            ysend[0, :, k:k + n, :] = ST[w, c, 2:18, 8 + y:8 + y + n, :]
            k += n
        rows = [(XY, 0, 1), (YZ, 0, 1), (YY, 0, 2), (XX, 0, 2), (XZ, 0, 2)]
        k = 8 * w
        for c, y, n in rows:
            ysend[1, :, k:k + n, :] = ST[w, c, 2:18, 8 + y:8 + y + n, :]
            k += n
    for e, x in ((0, 0), (1, 14)):
        bysend[0, e] = BU[2 + x:4 + x, 16:24, :]
        bysend[1, e] = BU[2 + x:4 + x, 8:16, :]

    def one(cond):
        return jnp.where(cond, 1, 0)

    peers = 2 + one(lower) + one(upper) + one(near_l) + one(near_r) + one(is3 | is4)
    pl.semaphore_wait(bar, peers)

    def remote(src, dst, ss, rs, dev):
        return pltpu.make_async_remote_copy(
            src_ref=src, dst_ref=dst, send_sem=ss, recv_sem=rs, device_id=dev, device_id_type=MESH
        )

    def x_copy(side, kind, j):
        src = (xs_send, xv_send)[kind].at[side, pl.ds(CHUNK * j, CHUNK)]
        dst = (xs_recv, xv_recv)[kind].at[side, pl.ds(CHUNK * j, CHUNK)]
        dev = (s, tx + 1 if side == 0 else tx - 1, ty)
        return remote(src, dst, x_ss.at[side, kind, j], x_rs.at[side, kind, j], dev)

    def to_relay(side, kind, j):
        src = (xs_send, xv_send)[kind].at[side, pl.ds(CHUNK * j, CHUNK)]
        dev = (s, j if side == 0 else 5 + j, ty)
        return remote(src, rel.at[kind], x_ss.at[side, kind, j], rel_rs.at[kind], dev)

    def relay_on(side, kind):
        j = tx if side == 0 else tx - 5
        dst = (xs_recv, xv_recv)[kind].at[side, pl.ds(CHUNK * j, CHUNK)]
        dev = (s, 4 if side == 0 else 3, ty)
        return remote(rel.at[kind], dst, rel_ss.at[kind], x_rs.at[side, kind, j], dev)

    near = (near_r, near_l)
    far = (is3, is4)
    exists_recv = (has_l, has_r)

    def send_x(kind):
        for side in range(2):
            @pl.when(far[side])
            def _():
                for j in range(3):
                    to_relay(side, kind, j).start()

            @pl.when(near[side])
            def _():
                for j in range(3):
                    x_copy(side, kind, j).start()

    exists_send_y = (upper, lower)
    exists_recv_y = (lower, upper)

    def y_copies(side):
        dev = (s, tx, ty + 1 if side == 0 else ty - 1)
        got = [remote(ysend.at[side], yrecv.at[side], y_ss.at[side, 0], y_rs.at[side, 0], dev)]
        for e in range(2):
            got.append(
                remote(bysend.at[side, e], byrecv.at[side, e], y_ss.at[side, 1 + e], y_rs.at[side, 1 + e], dev)
            )
        return got

    def y2_copy(side):
        dev = (s, tx, ty + 1 if side == 0 else ty - 1)
        src, dst = ((y2sb, y2rb), (y2sa, y2ra))[side]
        return remote(src, dst, y_ss.at[side, 3], y_rs.at[side, 3], dev)

    send_x(0)
    for side in range(2):
        @pl.when(exists_send_y[side])
        def _():
            for c in y_copies(side):
                c.start()

    relays = (low_relay, high_relay)
    for side in range(2):
        @pl.when(relays[side])
        def _():
            for kind in range(2):
                cp = relay_on(side, kind)
                to_relay(side, kind, 0).wait_recv()
                cp.start()

    for c in copies[7:]:
        c.wait()
    for side in range(2):
        @pl.when(exists_recv_y[side])
        def _():
            for c in y_copies(side):
                c.wait_recv()

    for w in range(2):
        k = 7 * w
        ST[w, XY, 2:18, 6:8, :] = yrecv[0, :, k:k + 2, :]
        ST[w, YZ, 2:18, 6:8, :] = yrecv[0, :, k + 2:k + 4, :]
        ST[w, YY, 2:18, 7:8, :] = yrecv[0, :, k + 4:k + 5, :]
        k = 8 * w
        ST[w, XY, 2:18, 24:25, :] = yrecv[1, :, k:k + 1, :]
        ST[w, YZ, 2:18, 24:25, :] = yrecv[1, :, k + 1:k + 2, :]
        ST[w, YY, 2:18, 24:26, :] = yrecv[1, :, k + 2:k + 4, :]

    zi = lax.broadcasted_iota(jnp.int32, (1, 1, 128), 2)
    up1 = (zi < 127).astype(F32)
    up2 = (zi < 126).astype(F32)
    dn1 = (zi > 0).astype(F32)
    dn2 = (zi > 1).astype(F32)

    def dpz(f):
        return (
            (C1 * up1) * pltpu.roll(f, 127, 2) - C1 * f
            + (C2 * up2) * pltpu.roll(f, 126, 2) - (C2 * dn1) * pltpu.roll(f, 1, 2)
        )

    def dmz(f):
        return (
            C1 * f - (C1 * dn1) * pltpu.roll(f, 1, 2)
            + (C2 * up1) * pltpu.roll(f, 127, 2) - (C2 * dn2) * pltpu.roll(f, 2, 2)
        )

    def getter(ref, w, x0, n):
        def get(c, dx=0, dy=0):
            return ref[w, c, pl.ds(2 + x0 + dx, n), 8 + dy:24 + dy, :]

        def dpx(c):
            return C1 * (get(c, 1) - get(c)) + C2 * (get(c, 2) - get(c, -1))

        def dmx(c):
            return C1 * (get(c) - get(c, -1)) + C2 * (get(c, 1) - get(c, -2))

        def dpy(c):
            return C1 * (get(c, 0, 1) - get(c)) + C2 * (get(c, 0, 2) - get(c, 0, -1))

        def dmy(c):
            return C1 * (get(c) - get(c, 0, -1)) + C2 * (get(c, 0, 1) - get(c, 0, -2))

        return get, dpx, dmx, dpy, dmy

    def accelerate(x0, n):
        scale = BU[pl.ds(2 + x0, n), 8:24, :]
        for w in range(2):
            get, dpx, dmx, dpy, dmy = getter(ST, w, x0, n)
            sums = (
                dpx(XX) + dmy(XY) + dmz(get(XZ)),
                dmx(XY) + dpy(YY) + dmz(get(YZ)),
                dmx(XZ) + dmy(YZ) + dpz(get(ZZ)),
            )
            for c in range(3):
                step = scale * sums[c]
                if w == 0:
                    AC[c, pl.ds(x0, n)] = step
                VE[w, c, pl.ds(2 + x0, n), 8:24, :] = VO[w, c, pl.ds(x0, n)] + step

    def accel_rows(i, carry):
        accelerate(2 * i, 2)
        return carry

    lax.fori_loop(0, 8, accel_rows, 0)

    for w in range(2):
        for i, (c, x) in enumerate([(0, 14), (0, 15), (1, 15), (2, 15)]):
            xv_send[0, 4 * w + i] = VE[w, c, 2 + x, 8:24, :]
        for i, (c, x) in enumerate([(0, 0), (1, 0), (1, 1), (2, 0), (2, 1)]):
            xv_send[1, 5 * w + i] = VE[w, c, 2 + x, 8:24, :]
        items = (
            [(XX, 15), (XY, 14), (XY, 15), (XZ, 14), (XZ, 15)],
            [(XX, 0), (XX, 1), (XY, 0), (XZ, 0)],
        )
        where = {XX: (5, 1, 4, 2), XY: (0, 2, 0, 1), XZ: (6, 1, 6, 2)}
        for side in range(2):
            for i, (c, x) in enumerate(items[side]):
                kb, nb, ka, na = where[c]
                xv_send[side, 10 + w, 3 * i:3 * i + nb, :] = yrecv[0, x, 7 * w + kb:7 * w + kb + nb, :]
                xv_send[side, 10 + w, 3 * i + nb:3 * i + 3, :] = yrecv[1, x, 8 * w + ka:8 * w + ka + na, :]
    send_x(1)
    for w in range(2):
        k = 4 * w
        for c, y, n in ((0, 15, 1), (1, 14, 2), (2, 15, 1)):
            y2sb[:, k:k + n, :] = VE[w, c, 2:18, 8 + y:8 + y + n, :]
            k += n
        k = 5 * w
        for c, y, n in ((0, 0, 2), (1, 0, 1), (2, 0, 2)):
            y2sa[:, k:k + n, :] = VE[w, c, 2:18, 8 + y:8 + y + n, :]
            k += n
    for side in range(2):
        @pl.when(exists_send_y[side])
        def _():
            y2_copy(side).start()
    for side in range(2):
        @pl.when(exists_recv_y[side])
        def _():
            y2_copy(side).wait_recv()
    for w in range(2):
        k = 4 * w
        for c, n in ((0, 1), (1, 2), (2, 1)):
            VE[w, c, 2:18, 8 - n:8, :] = y2rb[:, k:k + n, :]
            k += n
        k = 5 * w
        for c, n in ((0, 2), (1, 1), (2, 2)):
            VE[w, c, 2:18, 24:24 + n, :] = y2ra[:, k:k + n, :]
            k += n

    def finish(x0, n):
        lam = DT * LM[pl.ds(x0, n)]
        mu = DT * MU[pl.ds(x0, n)]
        rows = pl.ds(x0, n)
        kept = None
        for w, out in ((0, f_out), (1, a_out)):
            get, dpx, dmx, dpy, dmy = getter(VE, w, x0, n)
            vx, vy, vz = get(0), get(1), get(2)
            e = [
                dmx(0), dmy(1), dmz(vz),
                dpy(0) + dpx(1), dpz(vx) + dpx(2), dpz(vy) + dpy(2),
            ]
            trace = e[0] + e[1] + e[2]
            lt = lam * trace
            new = []
            for c in range(6):
                old = ST[w, c, pl.ds(2 + x0, n), 8:24, :]
                new.append(old + (lt + (2.0 * mu) * e[c]) if c < 3 else old + mu * e[c])
                out[3 + c, rows] = new[c]
            for c, v in enumerate((vx, vy, vz)):
                out[c, rows] = v
            if w == 0:
                kept = (trace, e)
            else:
                trace0, e0 = kept
                GL[0, rows] = (-DT) * trace0 * (new[0] + new[1] + new[2])
                prod = e0[0] * new[0]
                for c in range(1, 6):
                    prod = prod + e0[c] * new[c]
                GL[1, rows] = (-DT) * prod
                GL[2, rows] = -(AC[0, rows] * vx + AC[1, rows] * vy + AC[2, rows] * vz)

    def g_copy(k):
        lo, n = ((4, 8), (0, 4), (12, 4))[k]
        return remote(
            GL.at[:, pl.ds(lo, n)], GR.at[:, pl.ds(lo, n)], g_ss.at[k], g_rs.at[k], partner
        )

    def finish_rows(i, carry):
        finish(2 * i, 2)
        return carry

    lax.fori_loop(2, 6, finish_rows, 0)
    g_copy(0).start()

    def correct(w, c, x, e, terms):
        nb = 2 if c == 1 else 1
        layer, side = 10 + w, e
        lower_part = sum(k * xv_recv[side, layer, 3 * i:3 * i + nb, :] for i, k in terms)
        upper_part = sum(k * xv_recv[side, layer, 3 * i + nb:3 * i + 3, :] for i, k in terms)
        r = x if e == 0 else x - 14
        VE[w, c, 2 + x, 8 - nb:8, :] = VE[w, c, 2 + x, 8 - nb:8, :] + byrecv[0, e, r, 8 - nb:8, :] * lower_part
        na = 3 - nb
        VE[w, c, 2 + x, 24:24 + na, :] = VE[w, c, 2 + x, 24:24 + na, :] + byrecv[1, e, r, 0:na, :] * upper_part

    def edge(side):
        @pl.when(exists_recv[side])
        def _():
            for kind in range(2):
                for j in range(3):
                    x_copy(side, kind, j).wait_recv()

        def mine(w, c, x):
            return ST[w, c, 2 + x, 8:24, :]

        if side == 0:
            b2, b1 = xs_recv[0, 10], xs_recv[0, 11]
            for w in range(2):
                k = 5 * w
                ST[w, XX, 1, 8:24, :] = xs_recv[0, k]
                ST[w, XY, 0:2, 8:24, :] = xs_recv[0, k + 1:k + 3]
                ST[w, XZ, 0:2, 8:24, :] = xs_recv[0, k + 3:k + 5]
                k = 4 * w
                VE[w, 0, 0, 8:24, :] = xv_recv[0, k] + b2 * (C2 * mine(w, XX, 0))
                VE[w, 0, 1, 8:24, :] = xv_recv[0, k + 1] + b1 * (C1 * mine(w, XX, 0) + C2 * mine(w, XX, 1))
                VE[w, 1, 1, 8:24, :] = xv_recv[0, k + 2] + b1 * (C2 * mine(w, XY, 0))
                VE[w, 2, 1, 8:24, :] = xv_recv[0, k + 3] + b1 * (C2 * mine(w, XZ, 0))
                correct(w, 0, 0, 0, ((0, -C2),))
                correct(w, 1, 0, 0, ((2, -C1), (1, -C2)))
                correct(w, 1, 1, 0, ((2, -C2),))
                correct(w, 2, 0, 0, ((4, -C1), (3, -C2)))
                correct(w, 2, 1, 0, ((4, -C2),))
            accelerate(0, 2)
            first = 0
        else:
            b1, b2 = xs_recv[1, 8], xs_recv[1, 9]
            for w in range(2):
                k = 4 * w
                ST[w, XX, 18:20, 8:24, :] = xs_recv[1, k:k + 2]
                ST[w, XY, 18, 8:24, :] = xs_recv[1, k + 2]
                ST[w, XZ, 18, 8:24, :] = xs_recv[1, k + 3]
                k = 5 * w
                VE[w, 0, 18, 8:24, :] = xv_recv[1, k] - b1 * (C2 * mine(w, XX, 15))
                for c, st, at in ((1, XY, k + 1), (2, XZ, k + 3)):
                    VE[w, c, 18, 8:24, :] = xv_recv[1, at] - b1 * (C1 * mine(w, st, 15) + C2 * mine(w, st, 14))
                    VE[w, c, 19, 8:24, :] = xv_recv[1, at + 1] - b2 * (C2 * mine(w, st, 15))
                correct(w, 0, 14, 1, ((0, C2),))
                correct(w, 0, 15, 1, ((0, C1), (1, C2)))
                correct(w, 1, 15, 1, ((2, C2),))
                correct(w, 2, 15, 1, ((3, C2),))
            accelerate(14, 2)
            first = 6

        lax.fori_loop(first, first + 2, finish_rows, 0)
        g_copy(1 + side).start()

    @pl.when(jnp.logical_not(is4))
    def _():
        edge(0)

    edge(1)

    @pl.when(is4)
    def _():
        edge(0)

    for k, (lo, n) in enumerate(((4, 8), (0, 4), (12, 4))):
        g_copy(k).wait_recv()
        for c in range(3):
            g_out[c, lo:lo + n] = GL[c, lo:lo + n] + GR[c, lo:lo + n]

    for k in range(3):
        g_copy(k).wait_send()
    for side in range(2):
        @pl.when(exists_send_y[side])
        def _():
            for c in y_copies(side):
                c.wait_send()
            y2_copy(side).wait_send()

        @pl.when(near[side] | far[side])
        def _():
            for kind in range(2):
                for j in range(3):
                    x_copy(side, kind, j).wait_send()

        @pl.when(relays[side])
        def _():
            for kind in range(2):
                relay_on(side, kind).wait_send()


def store_kernel(f, a, g, f_out, a_out, g_out, sem):
    copies = [
        pltpu.make_async_copy(src, dst, sem.at[i])
        for i, (src, dst) in enumerate(((f, f_out), (a, a_out), (g, g_out)))
    ]
    for c in copies:
        c.start()
    for c in copies:
        c.wait()


def body(fwd, adj, lam, mu, den, scell, samp, rcell, ramp):
    fields, grads = (9, 16, 16, 128), (3, 16, 16, 128)
    hbm = pl.BlockSpec(memory_space=pltpu.HBM)
    vmem = pl.BlockSpec(memory_space=pltpu.VMEM)
    dma = pltpu.SemaphoreType.DMA

    def buf(*shape, dtype=F32):
        return pltpu.VMEM(shape, dtype)

    f, a, g = pl.pallas_call(
        step_kernel,
        out_shape=(pltpu.VMEM(fields, F32), pltpu.VMEM(fields, F32), pltpu.VMEM(grads, F32)),
        in_specs=[hbm] * 9,
        out_specs=(vmem, vmem, vmem),
        scratch_shapes=[
            buf(2, 6, 20, 32, 128), buf(2, 3, 20, 32, 128), buf(2, 3, 16, 16, 128), buf(3, 16, 16, 128),
            buf(20, 32, 128), buf(16, 16, 128), buf(16, 16, 128), buf(16, 16, 128),
            buf(1, 256, dtype=jnp.int32), buf(1, 256),
            pltpu.SMEM((1,), jnp.int32), pltpu.SMEM((1,), F32),
            buf(2, 16, 16, 128), buf(2, 16, 16, 128), buf(2, 2, 2, 8, 128), buf(2, 2, 2, 8, 128),
            buf(16, 8, 128), buf(16, 16, 128), buf(16, 8, 128), buf(16, 16, 128),
            buf(2, 12, 16, 128), buf(2, 12, 16, 128), buf(2, 12, 16, 128), buf(2, 12, 16, 128),
            buf(2, CHUNK, 16, 128), buf(3, 16, 16, 128), buf(3, 16, 16, 128),
            dma((11,)), dma((2, 4)), dma((2, 4)), dma((2, 2, 3)), dma((2, 2, 3)),
            dma((2,)), dma((2,)), dma((3,)), dma((3,)),
        ],
        compiler_params=pltpu.CompilerParams(
            collective_id=1, has_side_effects=True, vmem_limit_bytes=56 * 1024 * 1024
        ),
        name="step",
    )(fwd, adj, lam, mu, den, scell, samp, rcell, ramp)
    f, a, g = pl.pallas_call(
        store_kernel,
        out_shape=tuple(jax.ShapeDtypeStruct(shape, F32) for shape in (fields, fields, grads)),
        in_specs=[vmem] * 3,
        out_specs=(hbm,) * 3,
        scratch_shapes=[dma((3,))],
        compiler_params=pltpu.CompilerParams(vmem_limit_bytes=16 * 1024 * 1024),
        name="store",
    )(f, a, g)
    return f[None], a[None], g


def solution(mesh):
    fields = P("shot", None, "tx", "ty", None)
    grid = P("tx", "ty", None)
    return jax.shard_map(
        body,
        mesh=mesh,
        in_specs=(fields, fields, grid, grid, grid, P("shot"), P("shot"), P("shot", None), P("shot", None)),
        out_specs=(fields, fields, P(None, "tx", "ty", None)),
        check_vma=False,
    )
```

time: 156 us -> 37.8 us (0.24)
  the two profiles are of different devices: /device:TPU:1 before, /device:TPU:57 now
where the time goes in v1:
time: 37.8 us; the launch traced here: 37.6 us
  Pallas kernels  35.7 us (94%)
  between operations  1.93 us (5%)
    pallas_call x1, Pallas kernels, body(): pl.pallas_call(step_kernel, out_shape=(pltpu.VMEM(fields, F32), pltpu.VME...  34.1 us
    pallas_call x1, Pallas kernels, body(): pl.pallas_call(store_kernel, out_shape=tuple((jax.ShapeDtypeStruct(shape,...  1.55 us

profile of v1, /device:TPU:57, one launch (start us, length us, event | category | flops | bytes accessed | tf_op | source)
XLA Modules:
  0.0 37.6 jit_solution(15310398240771054360)
XLA Ops:
  1.9 34.1 %step.1 = (f32[9,16,16,128]{3,2,1,0:T(8,128)S(1)}, f32[9,16,16,128]{3,2,1,0:T(8,128)S(1)}, f32[3,16,16,128]{3,2,1,0:T(8,128)S(1)}) custom-call(f32[1,9,16,16,128]{4,3,2,1,0:T(8,128)} %fwd.1, f32[1,9,16,16,128]{4,3,2,1,0:T(8,128)} %adj.1, f32[16,16,128]{2,1,0:T(8,128)} %lam_h.1, f32[16,16,128]{2,1,0:T(8,128)} %mu_h.1, f32[16,16,128]{2,1,0:T(8,128)} %den_h.1, ...), custom_call_target="tpu_custom_call" | custom-call | tf_op jit(solution)/shard_map/step/pallas_call | solution.py:521
  36.1 1.6 %store.1 = (f32[9,16,16,128]{3,2,1,0:T(8,128)}, f32[9,16,16,128]{3,2,1,0:T(8,128)}, f32[3,16,16,128]{3,2,1,0:T(8,128)}) custom-call(f32[9,16,16,128]{3,2,1,0:T(8,128)S(1)} %get-tuple-element.9.f, f32[9,16,16,128]{3,2,1,0:T(8,128)S(1)} %get-tuple-element.10.a, f32[3,16,16,128]{3,2,1,0:T(8,128)S(1)} %get-tuple-element.11.g), custom_call_target="tpu_custom_call" | custom-call | tf_op jit(solution)/shard_map/store/pallas_call | solution.py:543

commit v2 on v1

--- a/solution.py
+++ b/solution.py
@@ -12,23 +12,21 @@
 DT = 0.15
 MESH = pl.DeviceIdType.MESH
 F32 = jnp.float32
-CHUNK = 4
 XX, YY, ZZ, XY, XZ, YZ = range(6)
 
 
 def step_kernel(
-    fwd, adj, lam_h, mu_h, den_h, scell_h, samp_h, rcell_h, ramp_h,
+    fwd, adj, lam_h, mu_h, den_h, source_h, rcell_h, ramp_h,
     f_out, a_out, g_out,
-    ST, VE, VO, AC, BU, LM, MU, ADD, rcell, ramp, scell, samp,
+    ST, VE, VO, AC, BU, LM, MU, ADD, rcell, ramp, source,
     ysend, yrecv, bysend, byrecv, y2sb, y2sa, y2rb, y2ra,
-    xs_send, xv_send, xs_recv, xv_recv, rel, GL, GR,
+    xs_send, xv_send, xe_send, xs_recv, xv_recv, xe_recv, rel_s, rel_v, GL, GR,
     in_sem, y_ss, y_rs, x_ss, x_rs, rel_ss, rel_rs, g_ss, g_rs,
 ):
     s, tx, ty = lax.axis_index("shot"), lax.axis_index("tx"), lax.axis_index("ty")
     last = lax.axis_size("ty") - 1
     partner = (1 - s, tx, ty)
 
-    has_l, has_r = tx > 0, tx < 7
     near_l, near_r = (tx > 0) & (tx != 4), (tx < 7) & (tx != 3)
     lower, upper = ty > 0, ty < last
     is3, is4 = tx == 3, tx == 4
@@ -41,9 +39,8 @@
         def _():
             pl.semaphore_signal(bar, inc=1, device_id=dev, device_id_type=MESH)
 
-    for j in range(3):
-        greet(is3, (s, 5 + j, ty))
-        greet(is4, (s, j, ty))
+    greet(is3, (s, 4, ty))
+    greet(is4, (s, 3, ty))
     greet(lower, (s, tx, ty - 1))
     greet(upper, (s, tx, ty + 1))
     greet(near_l, (s, tx - 1, ty))
@@ -57,8 +54,7 @@
         (adj.at[0, pl.ds(3, 6)], ST.at[1, :, pl.ds(2, 16), pl.ds(8, 16)]),
         (rcell_h, rcell),
         (ramp_h, ramp),
-        (scell_h, scell),
-        (samp_h, samp),
+        (source_h, source),
         (den_h, BU.at[pl.ds(2, 16), pl.ds(8, 16)]),
         (fwd.at[0, pl.ds(0, 3)], VO.at[0]),
         (adj.at[0, pl.ds(0, 3)], VO.at[1]),
@@ -86,15 +82,16 @@
     for side, gone in ((0, tx == 0), (1, tx == 7)):
         clear(gone, xs_recv, side)
         clear(gone, xv_recv, side)
-    xs_send[1, 10:12] = jnp.zeros((2, 16, 128), F32)
-    xv_send[0, 8:10] = jnp.zeros((2, 16, 128), F32)
-    for side in range(2):
-        for w in range(2):
-            xv_send[side, 10 + w] = jnp.zeros((16, 128), F32)
+        clear(gone, xe_recv, side)
+    xe_send[...] = jnp.zeros(xe_send.shape, F32)
+    for w in range(2):
+        for c in (XY, YY, YZ):
+            for lo in (0, 24):
+                ST[w, c, 2:18, lo:lo + 8, :] = jnp.zeros((16, 8, 128), F32)
     ysend[0, :, 8:16, :] = jnp.zeros((16, 8, 128), F32)
     y2sa[:, 8:16, :] = jnp.zeros((16, 8, 128), F32)
 
-    for c in copies[2:6]:
+    for c in copies[2:5]:
         c.wait()
 
     def place(cell):
@@ -115,17 +112,15 @@
         lax.dot_general(hot, part, nt, preferred_element_type=F32) for part in (low, mid, high)
     )
     ADD[...] = added.reshape(16, 16, 128)
-    scol, sdep = place(scell[0])
-    ssum = samp[0]
     copies[0].wait()
     copies[1].wait()
 
     def inject_rows(i, carry):
         shape = (2, 16, 128)
-        col = (lax.broadcasted_iota(jnp.int32, shape, 0) + 2 * i) * 16 + lax.broadcasted_iota(jnp.int32, shape, 1)
-        dep = lax.broadcasted_iota(jnp.int32, shape, 2)
-        hit = (col == scol) & (dep == sdep)
-        src = jnp.where(hit, ssum, 0.0)
+        gx = lax.broadcasted_iota(jnp.int32, shape, 0) + (2 * i + tx * 16)
+        gy = lax.broadcasted_iota(jnp.int32, shape, 1) + ty * 16
+        cell = gx * 65536 + gy * 128 + lax.broadcasted_iota(jnp.int32, shape, 2)
+        src = jnp.where(cell.astype(F32) == source[0], source[1], 0.0)
         rows = pl.ds(2 + 2 * i, 2)
         for c in range(3):
             ST[0, c, rows, 8:24, :] = ST[0, c, rows, 8:24, :] + src
@@ -133,7 +128,7 @@
         return carry
 
     lax.fori_loop(0, 8, inject_rows, 0)
-    copies[6].wait()
+    copies[5].wait()
     BU[2:18, 8:24, :] = DT / BU[2:18, 8:24, :]
 
     for w in range(2):
@@ -144,7 +139,7 @@
         for i, (c, x) in enumerate(layers):
             xs_send[1, 4 * w + i] = ST[w, c, 2 + x, 8:24, :]
     for i in range(2):
-        xs_send[0, 10 + i] = BU[16 + i, 8:24, :]
+        xv_send[0, 8 + i] = BU[16 + i, 8:24, :]
         xs_send[1, 8 + i] = BU[2 + i, 8:24, :]
     for w in range(2):
         rows = [(XY, 14, 2), (YZ, 14, 2), (YY, 15, 1), (XX, 15, 1), (XZ, 15, 1)]
@@ -160,101 +155,6 @@
     for e, x in ((0, 0), (1, 14)):
         bysend[0, e] = BU[2 + x:4 + x, 16:24, :]
         bysend[1, e] = BU[2 + x:4 + x, 8:16, :]
-
-    def one(cond):
-        return jnp.where(cond, 1, 0)
-
-    peers = 2 + one(lower) + one(upper) + one(near_l) + one(near_r) + one(is3 | is4)
-    pl.semaphore_wait(bar, peers)
-
-    def remote(src, dst, ss, rs, dev):
-        return pltpu.make_async_remote_copy(
-            src_ref=src, dst_ref=dst, send_sem=ss, recv_sem=rs, device_id=dev, device_id_type=MESH
-        )
-
-    def x_copy(side, kind, j):
-        src = (xs_send, xv_send)[kind].at[side, pl.ds(CHUNK * j, CHUNK)]
-        dst = (xs_recv, xv_recv)[kind].at[side, pl.ds(CHUNK * j, CHUNK)]
-        dev = (s, tx + 1 if side == 0 else tx - 1, ty)
-        return remote(src, dst, x_ss.at[side, kind, j], x_rs.at[side, kind, j], dev)
-
-    def to_relay(side, kind, j):
-        src = (xs_send, xv_send)[kind].at[side, pl.ds(CHUNK * j, CHUNK)]
-        dev = (s, j if side == 0 else 5 + j, ty)
-        return remote(src, rel.at[kind], x_ss.at[side, kind, j], rel_rs.at[kind], dev)
-
-    def relay_on(side, kind):
-        j = tx if side == 0 else tx - 5
-        dst = (xs_recv, xv_recv)[kind].at[side, pl.ds(CHUNK * j, CHUNK)]
-        dev = (s, 4 if side == 0 else 3, ty)
-        return remote(rel.at[kind], dst, rel_ss.at[kind], x_rs.at[side, kind, j], dev)
-
-    near = (near_r, near_l)
-    far = (is3, is4)
-    exists_recv = (has_l, has_r)
-
-    def send_x(kind):
-        for side in range(2):
-            @pl.when(far[side])
-            def _():
-                for j in range(3):
-                    to_relay(side, kind, j).start()
-
-            @pl.when(near[side])
-            def _():
-                for j in range(3):
-                    x_copy(side, kind, j).start()
-
-    exists_send_y = (upper, lower)
-    exists_recv_y = (lower, upper)
-
-    def y_copies(side):
-        dev = (s, tx, ty + 1 if side == 0 else ty - 1)
-        got = [remote(ysend.at[side], yrecv.at[side], y_ss.at[side, 0], y_rs.at[side, 0], dev)]
-        for e in range(2):
-            got.append(
-                remote(bysend.at[side, e], byrecv.at[side, e], y_ss.at[side, 1 + e], y_rs.at[side, 1 + e], dev)
-            )
-        return got
-
-    def y2_copy(side):
-        dev = (s, tx, ty + 1 if side == 0 else ty - 1)
-        src, dst = ((y2sb, y2rb), (y2sa, y2ra))[side]
-        return remote(src, dst, y_ss.at[side, 3], y_rs.at[side, 3], dev)
-
-    send_x(0)
-    for side in range(2):
-        @pl.when(exists_send_y[side])
-        def _():
-            for c in y_copies(side):
-                c.start()
-
-    relays = (low_relay, high_relay)
-    for side in range(2):
-        @pl.when(relays[side])
-        def _():
-            for kind in range(2):
-                cp = relay_on(side, kind)
-                to_relay(side, kind, 0).wait_recv()
-                cp.start()
-
-    for c in copies[7:]:
-        c.wait()
-    for side in range(2):
-        @pl.when(exists_recv_y[side])
-        def _():
-            for c in y_copies(side):
-                c.wait_recv()
-
-    for w in range(2):
-        k = 7 * w
-        ST[w, XY, 2:18, 6:8, :] = yrecv[0, :, k:k + 2, :]
-        ST[w, YZ, 2:18, 6:8, :] = yrecv[0, :, k + 2:k + 4, :]
-        ST[w, YY, 2:18, 7:8, :] = yrecv[0, :, k + 4:k + 5, :]
-        k = 8 * w
-        ST[w, XY, 2:18, 24:25, :] = yrecv[1, :, k:k + 1, :]
-        ST[w, YZ, 2:18, 24:25, :] = yrecv[1, :, k + 1:k + 2, :]
-        ST[w, YY, 2:18, 24:26, :] = yrecv[1, :, k + 2:k + 4, :]
 
     zi = lax.broadcasted_iota(jnp.int32, (1, 1, 128), 2)
     up1 = (zi < 127).astype(F32)
@@ -307,28 +207,148 @@
                     AC[c, pl.ds(x0, n)] = step
                 VE[w, c, pl.ds(2 + x0, n), 8:24, :] = VO[w, c, pl.ds(x0, n)] + step
 
-    def accel_rows(i, carry):
-        accelerate(2 * i, 2)
-        return carry
-
-    lax.fori_loop(0, 8, accel_rows, 0)
+    for c in copies[6:]:
+        c.wait()
+    accelerate(0, 2)
+    accelerate(14, 2)
 
     for w in range(2):
         for i, (c, x) in enumerate([(0, 14), (0, 15), (1, 15), (2, 15)]):
             xv_send[0, 4 * w + i] = VE[w, c, 2 + x, 8:24, :]
         for i, (c, x) in enumerate([(0, 0), (1, 0), (1, 1), (2, 0), (2, 1)]):
             xv_send[1, 5 * w + i] = VE[w, c, 2 + x, 8:24, :]
-        items = (
-            [(XX, 15), (XY, 14), (XY, 15), (XZ, 14), (XZ, 15)],
-            [(XX, 0), (XX, 1), (XY, 0), (XZ, 0)],
-        )
-        where = {XX: (5, 1, 4, 2), XY: (0, 2, 0, 1), XZ: (6, 1, 6, 2)}
+
+    def one(cond):
+        return jnp.where(cond, 1, 0)
+
+    far_end = is3 | is4
+    peers = 1 + one(lower) + one(upper) + one(near_l) + one(near_r) + 3 * one(far_end)
+    pl.semaphore_wait(bar, peers)
+
+    def remote(src, dst, ss, rs, dev):
+        return pltpu.make_async_remote_copy(
+            src_ref=src, dst_ref=dst, send_sem=ss, recv_sem=rs, device_id=dev, device_id_type=MESH
+        )
+
+    x_send = (xs_send, xv_send, xe_send)
+    x_recv = (xs_recv, xv_recv, xe_recv)
+    relay_buf = (rel_s, rel_v)
+
+    def layers_of(kind, j):
+        if j is None:
+            return (pl.ds(0, 4), pl.ds(9, 1))[kind]
+        return (pl.ds(4 + 2 * j, 2), pl.ds(3 * j, 3))[kind]
+
+    def x_near(side, kind):
+        dev = (s, tx + 1 if side == 0 else tx - 1, ty)
+        return remote(
+            x_send[kind].at[side], x_recv[kind].at[side], x_ss.at[side, kind, 0], x_rs.at[side, kind, 0], dev
+        )
+
+    def x_straight(side, kind):
+        dev = (s, 4 if side == 0 else 3, ty)
+        part = layers_of(kind, None)
+        return remote(
+            x_send[kind].at[side, part], x_recv[kind].at[side, part],
+            x_ss.at[side, kind, 0], x_rs.at[side, kind, 0], dev,
+        )
+
+    def to_relay(side, kind, j):
+        dev = (s, j if side == 0 else 5 + j, ty)
+        return remote(
+            x_send[kind].at[side, layers_of(kind, j)], relay_buf[kind],
+            x_ss.at[side, kind, 1 + j], rel_rs.at[kind], dev,
+        )
+
+    def relay_on(side, kind, j):
+        dev = (s, 4 if side == 0 else 3, ty)
+        return remote(
+            relay_buf[kind], x_recv[kind].at[side, layers_of(kind, j)],
+            rel_ss.at[kind], x_rs.at[side, kind, 1 + j], dev,
+        )
+
+    near = (near_r, near_l)
+    far = (is3, is4)
+    near_recv = (near_l, near_r)
+    far_recv = (is4, is3)
+
+    def far_copies(side, kind):
+        if kind == 2:
+            return [x_near(side, 2)]
+        return [to_relay(side, kind, j) for j in range(3)] + [x_straight(side, kind)]
+
+    def send_x(kind):
         for side in range(2):
+            @pl.when(far[side])
+            def _():
+                for cp in far_copies(side, kind):
+                    cp.start()
+
+            @pl.when(near[side])
+            def _():
+                x_near(side, kind).start()
+
+    exists_send_y = (upper, lower)
+    exists_recv_y = (lower, upper)
+
+    def y_copies(side):
+        dev = (s, tx, ty + 1 if side == 0 else ty - 1)
+        got = [remote(ysend.at[side], yrecv.at[side], y_ss.at[side, 0], y_rs.at[side, 0], dev)]
+        for e in range(2):
+            got.append(
+                remote(bysend.at[side, e], byrecv.at[side, e], y_ss.at[side, 1 + e], y_rs.at[side, 1 + e], dev)
+            )
+        return got
+
+    def y2_copy(side):
+        dev = (s, tx, ty + 1 if side == 0 else ty - 1)
+        src, dst = ((y2sb, y2rb), (y2sa, y2ra))[side]
+        return remote(src, dst, y_ss.at[side, 3], y_rs.at[side, 3], dev)
+
+    send_x(0)
+    send_x(1)
+    for side in range(2):
+        @pl.when(exists_send_y[side])
+        def _():
+            for c in y_copies(side):
+                c.start()
+
+
+    for side in range(2):
+        @pl.when(exists_recv_y[side])
+        def _():
+            for c in y_copies(side):
+                c.wait_recv()
+
+    for w in range(2):
+        k = 7 * w
+        ST[w, XY, 2:18, 6:8, :] = yrecv[0, :, k:k + 2, :]
+        ST[w, YZ, 2:18, 6:8, :] = yrecv[0, :, k + 2:k + 4, :]
+        ST[w, YY, 2:18, 7:8, :] = yrecv[0, :, k + 4:k + 5, :]
+        k = 8 * w
+        ST[w, XY, 2:18, 24:25, :] = yrecv[1, :, k:k + 1, :]
+        ST[w, YZ, 2:18, 24:25, :] = yrecv[1, :, k + 1:k + 2, :]
+        ST[w, YY, 2:18, 24:26, :] = yrecv[1, :, k + 2:k + 4, :]
+
+    items = (
+        [(XX, 15), (XY, 14), (XY, 15), (XZ, 14), (XZ, 15), (YY, 15), (YZ, 15)],
+        [(XX, 0), (XX, 1), (XY, 0), (XZ, 0), (YY, 0), (YY, 1), (YZ, 0), (YZ, 1)],
+    )
+    where = {XX: (5, 1, 4, 2), XY: (0, 2, 0, 1), XZ: (6, 1, 6, 2), YY: (4, 1, 2, 2), YZ: (2, 2, 1, 1)}
+    for side in range(2):
+        for w in range(2):
             for i, (c, x) in enumerate(items[side]):
                 kb, nb, ka, na = where[c]
-                xv_send[side, 10 + w, 3 * i:3 * i + nb, :] = yrecv[0, x, 7 * w + kb:7 * w + kb + nb, :]
-                xv_send[side, 10 + w, 3 * i + nb:3 * i + 3, :] = yrecv[1, x, 8 * w + ka:8 * w + ka + na, :]
-    send_x(1)
+                xe_send[side, w, 3 * i:3 * i + nb, :] = yrecv[0, x, 7 * w + kb:7 * w + kb + nb, :]
+                xe_send[side, w, 3 * i + nb:3 * i + 3, :] = yrecv[1, x, 8 * w + ka:8 * w + ka + na, :]
+    send_x(2)
+
+    def accel_rows(i, carry):
+        accelerate(2 * i, 2)
+        return carry
+
+    lax.fori_loop(0, 8, accel_rows, 0)
+
     for w in range(2):
         k = 4 * w
         for c, y, n in ((0, 15, 1), (1, 14, 2), (2, 15, 1)):
@@ -342,6 +362,15 @@
         @pl.when(exists_send_y[side])
         def _():
             y2_copy(side).start()
+    relays = (low_relay, high_relay)
+    for side in range(2):
+        @pl.when(relays[side])
+        def _():
+            j = tx if side == 0 else tx - 5
+            for kind in range(2):
+                to_relay(side, kind, 0).wait_recv()
+                relay_on(side, kind, j).start()
+
     for side in range(2):
         @pl.when(exists_recv_y[side])
         def _():
@@ -403,26 +432,43 @@
 
     def correct(w, c, x, e, terms):
         nb = 2 if c == 1 else 1
-        layer, side = 10 + w, e
-        lower_part = sum(k * xv_recv[side, layer, 3 * i:3 * i + nb, :] for i, k in terms)
-        upper_part = sum(k * xv_recv[side, layer, 3 * i + nb:3 * i + 3, :] for i, k in terms)
+        lower_part = sum(k * xe_recv[e, w, 3 * i:3 * i + nb, :] for i, k in terms)
+        upper_part = sum(k * xe_recv[e, w, 3 * i + nb:3 * i + 3, :] for i, k in terms)
         r = x if e == 0 else x - 14
         VE[w, c, 2 + x, 8 - nb:8, :] = VE[w, c, 2 + x, 8 - nb:8, :] + byrecv[0, e, r, 8 - nb:8, :] * lower_part
         na = 3 - nb
         VE[w, c, 2 + x, 24:24 + na, :] = VE[w, c, 2 + x, 24:24 + na, :] + byrecv[1, e, r, 0:na, :] * upper_part
 
+    def rim(w, c, x, e, scale, i, forward):
+        def f(k):
+            return xe_recv[e, w, 3 * i + k:3 * i + k + 1, :]
+
+        if forward:
+            adds = ((0, -C2 * f(0)), (14, C2 * f(1)), (15, C1 * f(1) + C2 * f(2)))
+        else:
+            adds = ((0, -C1 * f(1) - C2 * f(0)), (1, -C2 * f(1)), (15, C2 * f(2)))
+        for y, v in adds:
+            VE[w, c, x, 8 + y:9 + y, :] = VE[w, c, x, 8 + y:9 + y, :] + scale[y:y + 1, :] * v
+
     def edge(side):
-        @pl.when(exists_recv[side])
+        @pl.when(near_recv[side])
+        def _():
+            for kind in range(3):
+                x_near(side, kind).wait_recv()
+
+        @pl.when(far_recv[side])
         def _():
             for kind in range(2):
                 for j in range(3):
-                    x_copy(side, kind, j).wait_recv()
+                    relay_on(side, kind, j).wait_recv()
+                x_straight(side, kind).wait_recv()
+            x_near(side, 2).wait_recv()
 
         def mine(w, c, x):
             return ST[w, c, 2 + x, 8:24, :]
 
         if side == 0:
-            b2, b1 = xs_recv[0, 10], xs_recv[0, 11]
+            b2, b1 = xv_recv[0, 8], xv_recv[0, 9]
             for w in range(2):
                 k = 5 * w
                 ST[w, XX, 1, 8:24, :] = xs_recv[0, k]
@@ -433,6 +479,10 @@
                 VE[w, 0, 1, 8:24, :] = xv_recv[0, k + 1] + b1 * (C1 * mine(w, XX, 0) + C2 * mine(w, XX, 1))
                 VE[w, 1, 1, 8:24, :] = xv_recv[0, k + 2] + b1 * (C2 * mine(w, XY, 0))
                 VE[w, 2, 1, 8:24, :] = xv_recv[0, k + 3] + b1 * (C2 * mine(w, XZ, 0))
+                rim(w, 0, 0, 0, xv_recv.at[0, 8], 1, False)
+                rim(w, 0, 1, 0, xv_recv.at[0, 9], 2, False)
+                rim(w, 1, 1, 0, xv_recv.at[0, 9], 5, True)
+                rim(w, 2, 1, 0, xv_recv.at[0, 9], 6, False)
                 correct(w, 0, 0, 0, ((0, -C2),))
                 correct(w, 1, 0, 0, ((2, -C1), (1, -C2)))
                 correct(w, 1, 1, 0, ((2, -C2),))
@@ -452,6 +502,11 @@
                 for c, st, at in ((1, XY, k + 1), (2, XZ, k + 3)):
                     VE[w, c, 18, 8:24, :] = xv_recv[1, at] - b1 * (C1 * mine(w, st, 15) + C2 * mine(w, st, 14))
                     VE[w, c, 19, 8:24, :] = xv_recv[1, at + 1] - b2 * (C2 * mine(w, st, 15))
+                rim(w, 0, 18, 1, xs_recv.at[1, 8], 2, False)
+                rim(w, 1, 18, 1, xs_recv.at[1, 8], 4, True)
+                rim(w, 1, 19, 1, xs_recv.at[1, 9], 5, True)
+                rim(w, 2, 18, 1, xs_recv.at[1, 8], 6, False)
+                rim(w, 2, 19, 1, xs_recv.at[1, 9], 7, False)
                 correct(w, 0, 14, 1, ((0, C2),))
                 correct(w, 0, 15, 1, ((0, C1), (1, C2)))
                 correct(w, 1, 15, 1, ((2, C2),))
@@ -486,16 +541,21 @@
                 c.wait_send()
             y2_copy(side).wait_send()
 
-        @pl.when(near[side] | far[side])
+        @pl.when(near[side])
+        def _():
+            for kind in range(3):
+                x_near(side, kind).wait_send()
+
+        @pl.when(far[side])
+        def _():
+            for kind in range(3):
+                for cp in far_copies(side, kind):
+                    cp.wait_send()
+
+        @pl.when(relays[side])
         def _():
             for kind in range(2):
-                for j in range(3):
-                    x_copy(side, kind, j).wait_send()
-
-        @pl.when(relays[side])
-        def _():
-            for kind in range(2):
-                relay_on(side, kind).wait_send()
+                relay_on(side, kind, 0).wait_send()
 
 
 def store_kernel(f, a, g, f_out, a_out, g_out, sem):
@@ -515,31 +575,34 @@
     vmem = pl.BlockSpec(memory_space=pltpu.VMEM)
     dma = pltpu.SemaphoreType.DMA
 
+    source = jnp.concatenate([scell.astype(F32), samp])
+
     def buf(*shape, dtype=F32):
         return pltpu.VMEM(shape, dtype)
 
     f, a, g = pl.pallas_call(
         step_kernel,
         out_shape=(pltpu.VMEM(fields, F32), pltpu.VMEM(fields, F32), pltpu.VMEM(grads, F32)),
-        in_specs=[hbm] * 9,
+        in_specs=[hbm] * 8,
         out_specs=(vmem, vmem, vmem),
         scratch_shapes=[
             buf(2, 6, 20, 32, 128), buf(2, 3, 20, 32, 128), buf(2, 3, 16, 16, 128), buf(3, 16, 16, 128),
             buf(20, 32, 128), buf(16, 16, 128), buf(16, 16, 128), buf(16, 16, 128),
             buf(1, 256, dtype=jnp.int32), buf(1, 256),
-            pltpu.SMEM((1,), jnp.int32), pltpu.SMEM((1,), F32),
+            pltpu.SMEM((2,), F32),
             buf(2, 16, 16, 128), buf(2, 16, 16, 128), buf(2, 2, 2, 8, 128), buf(2, 2, 2, 8, 128),
             buf(16, 8, 128), buf(16, 16, 128), buf(16, 8, 128), buf(16, 16, 128),
-            buf(2, 12, 16, 128), buf(2, 12, 16, 128), buf(2, 12, 16, 128), buf(2, 12, 16, 128),
-            buf(2, CHUNK, 16, 128), buf(3, 16, 16, 128), buf(3, 16, 16, 128),
-            dma((11,)), dma((2, 4)), dma((2, 4)), dma((2, 2, 3)), dma((2, 2, 3)),
+            buf(2, 10, 16, 128), buf(2, 10, 16, 128), buf(2, 2, 24, 128),
+            buf(2, 10, 16, 128), buf(2, 10, 16, 128), buf(2, 2, 24, 128),
+            buf(2, 16, 128), buf(3, 16, 128), buf(3, 16, 16, 128), buf(3, 16, 16, 128),
+            dma((10,)), dma((2, 4)), dma((2, 4)), dma((2, 3, 4)), dma((2, 3, 4)),
             dma((2,)), dma((2,)), dma((3,)), dma((3,)),
         ],
         compiler_params=pltpu.CompilerParams(
             collective_id=1, has_side_effects=True, vmem_limit_bytes=56 * 1024 * 1024
         ),
         name="step",
-    )(fwd, adj, lam, mu, den, scell, samp, rcell, ramp)
+    )(fwd, adj, lam, mu, den, source, rcell, ramp)
     f, a, g = pl.pallas_call(
         store_kernel,
         out_shape=tuple(jax.ShapeDtypeStruct(shape, F32) for shape in (fields, fields, grads)),

time: 37.8 us -> 36.9 us (0.976)
  the two profiles are of different devices: /device:TPU:57 before, /device:TPU:127 now
where the time goes in v2:
time: 36.9 us; the launch traced here: 36.8 us
  Pallas kernels  34.3 us (93%)
  between operations  1.93 us (5%)
  other arithmetic  0.59 us (2%)
    pallas_call x1, Pallas kernels, body(): pl.pallas_call(step_kernel, out_shape=(pltpu.VMEM(fields, F32), pltpu.VME...  32.7 us
    pallas_call x1, Pallas kernels, body(): pl.pallas_call(store_kernel, out_shape=tuple((jax.ShapeDtypeStruct(shape,...  1.55 us

profile of v2, /device:TPU:127, one launch (start us, length us, event | category | flops | bytes accessed | tf_op | source)
XLA Modules:
  0.0 36.8 jit_solution(5122372696361331590)
XLA Ops:
  1.9 0.6 %pad_maximum_fusion.source_h = f32[2]{0:T(128)} fusion(f32[1]{0:T(128)S(6)} %copy.13, f32[1]{0:T(128)S(6)} %convert_element_type.3), kind=kLoop, calls=%fused_computation | loop fusion | flops 2 | bytes 16 | tf_op jit(solution)/shard_map/concatenate | solution.py:578
  2.5 32.7 %step.1 = (f32[9,16,16,128]{3,2,1,0:T(8,128)S(1)}, f32[9,16,16,128]{3,2,1,0:T(8,128)S(1)}, f32[3,16,16,128]{3,2,1,0:T(8,128)S(1)}) custom-call(f32[1,9,16,16,128]{4,3,2,1,0:T(8,128)} %fwd.1, f32[1,9,16,16,128]{4,3,2,1,0:T(8,128)} %adj.1, f32[16,16,128]{2,1,0:T(8,128)} %lam_h.1, f32[16,16,128]{2,1,0:T(8,128)} %mu_h.1, f32[16,16,128]{2,1,0:T(8,128)} %den_h.1, ...), custom_call_target="tpu_custom_call" | custom-call | tf_op jit(solution)/shard_map/step/pallas_call | solution.py:583
  35.2 1.6 %store.1 = (f32[9,16,16,128]{3,2,1,0:T(8,128)}, f32[9,16,16,128]{3,2,1,0:T(8,128)}, f32[3,16,16,128]{3,2,1,0:T(8,128)}) custom-call(f32[9,16,16,128]{3,2,1,0:T(8,128)S(1)} %get-tuple-element.9.f, f32[9,16,16,128]{3,2,1,0:T(8,128)S(1)} %get-tuple-element.10.a, f32[3,16,16,128]{3,2,1,0:T(8,128)S(1)} %get-tuple-element.11.g), custom_call_target="tpu_custom_call" | custom-call | tf_op jit(solution)/shard_map/store/pallas_call | solution.py:606

commit v3 on v2

--- a/solution.py
+++ b/solution.py
@@ -19,7 +19,7 @@
     fwd, adj, lam_h, mu_h, den_h, source_h, rcell_h, ramp_h,
     f_out, a_out, g_out,
     ST, VE, VO, AC, BU, LM, MU, ADD, rcell, ramp, source,
-    ysend, yrecv, bysend, byrecv, y2sb, y2sa, y2rb, y2ra,
+    ysend, yrecv, rimsend, rimrecv, y2sb, y2sa, y2rb, y2ra,
     xs_send, xv_send, xe_send, xs_recv, xv_recv, xe_recv, rel_s, rel_v, GL, GR,
     in_sem, y_ss, y_rs, x_ss, x_rs, rel_ss, rel_rs, g_ss, g_rs,
 ):
@@ -76,7 +76,7 @@
                 ST[w, c, lo:lo + 2, 8:24, :] = jnp.zeros((2, 16, 128), F32)
     for side, gone in ((0, ty == 0), (1, ty == last)):
         clear(gone, yrecv, side)
-        clear(gone, byrecv, side)
+        clear(gone, rimrecv, side)
     clear(ty == 0, y2rb, slice(None))
     clear(ty == last, y2ra, slice(None))
     for side, gone in ((0, tx == 0), (1, tx == 7)):
@@ -88,8 +88,7 @@
         for c in (XY, YY, YZ):
             for lo in (0, 24):
                 ST[w, c, 2:18, lo:lo + 8, :] = jnp.zeros((16, 8, 128), F32)
-    ysend[0, :, 8:16, :] = jnp.zeros((16, 8, 128), F32)
-    y2sa[:, 8:16, :] = jnp.zeros((16, 8, 128), F32)
+    rimsend[0, 0:4] = jnp.zeros((4, 8, 128), F32)
 
     for c in copies[2:5]:
         c.wait()
@@ -141,20 +140,28 @@
     for i in range(2):
         xv_send[0, 8 + i] = BU[16 + i, 8:24, :]
         xs_send[1, 8 + i] = BU[2 + i, 8:24, :]
-    for w in range(2):
-        rows = [(XY, 14, 2), (YZ, 14, 2), (YY, 15, 1), (XX, 15, 1), (XZ, 15, 1)]
-        k = 7 * w
-        for c, y, n in rows:
-            ysend[0, :, k:k + n, :] = ST[w, c, 2:18, 8 + y:8 + y + n, :]
+    edges = (0, 1, 14, 15)
+    for w in range(2):
+        k = 4 * w
+        for c, y, n in ((XY, 14, 2), (YZ, 14, 2)):
+            ysend[0, 0:16, k:k + n, :] = ST[w, c, 2:18, 8 + y:8 + y + n, :]
             k += n
-        rows = [(XY, 0, 1), (YZ, 0, 1), (YY, 0, 2), (XX, 0, 2), (XZ, 0, 2)]
-        k = 8 * w
-        for c, y, n in rows:
-            ysend[1, :, k:k + n, :] = ST[w, c, 2:18, 8 + y:8 + y + n, :]
+        for x in range(16):
+            k = 16 * w + x
+            ysend[0, 16 + k // 8, k % 8:k % 8 + 1, :] = ST[w, YY, 2 + x, 23:24, :]
+        k = 4 * w
+        for c, n in ((XY, 1), (YZ, 1), (YY, 2)):
+            ysend[1, 0:16, k:k + n, :] = ST[w, c, 2:18, 8:8 + n, :]
             k += n
-    for e, x in ((0, 0), (1, 14)):
-        bysend[0, e] = BU[2 + x:4 + x, 16:24, :]
-        bysend[1, e] = BU[2 + x:4 + x, 8:16, :]
+        for i, x in enumerate(edges):
+            for q, c in enumerate((XX, XZ)):
+                k = 2 * w + q
+                rimsend[0, i, k:k + 1, :] = ST[w, c, 2 + x, 23:24, :]
+                k = 4 * w + 2 * q
+                rimsend[1, i, k:k + 2, :] = ST[w, c, 2 + x, 8:10, :]
+    for i, x in enumerate(edges):
+        rimsend[0, 4 + i] = BU[2 + x, 16:24, :]
+        rimsend[1, 4 + i] = BU[2 + x, 8:16, :]
 
     zi = lax.broadcasted_iota(jnp.int32, (1, 1, 128), 2)
     up1 = (zi < 127).astype(F32)
@@ -291,77 +298,94 @@
     exists_send_y = (upper, lower)
     exists_recv_y = (lower, upper)
 
-    def y_copies(side):
+    def y_copy(side):
         dev = (s, tx, ty + 1 if side == 0 else ty - 1)
-        got = [remote(ysend.at[side], yrecv.at[side], y_ss.at[side, 0], y_rs.at[side, 0], dev)]
-        for e in range(2):
-            got.append(
-                remote(bysend.at[side, e], byrecv.at[side, e], y_ss.at[side, 1 + e], y_rs.at[side, 1 + e], dev)
-            )
-        return got
+        part = pl.ds(0, 20) if side == 0 else pl.ds(0, 16)
+        return remote(ysend.at[side, part], yrecv.at[side, part], y_ss.at[side, 0], y_rs.at[side, 0], dev)
+
+    def rim_copy(side):
+        dev = (s, tx, ty + 1 if side == 0 else ty - 1)
+        return remote(rimsend.at[side], rimrecv.at[side], y_ss.at[side, 1], y_rs.at[side, 1], dev)
 
     def y2_copy(side):
         dev = (s, tx, ty + 1 if side == 0 else ty - 1)
         src, dst = ((y2sb, y2rb), (y2sa, y2ra))[side]
         return remote(src, dst, y_ss.at[side, 3], y_rs.at[side, 3], dev)
 
+    for side in range(2):
+        @pl.when(exists_send_y[side])
+        def _():
+            y_copy(side).start()
     send_x(0)
     send_x(1)
     for side in range(2):
         @pl.when(exists_send_y[side])
         def _():
-            for c in y_copies(side):
-                c.start()
+            rim_copy(side).start()
 
 
     for side in range(2):
         @pl.when(exists_recv_y[side])
         def _():
-            for c in y_copies(side):
-                c.wait_recv()
-
-    for w in range(2):
-        k = 7 * w
-        ST[w, XY, 2:18, 6:8, :] = yrecv[0, :, k:k + 2, :]
-        ST[w, YZ, 2:18, 6:8, :] = yrecv[0, :, k + 2:k + 4, :]
-        ST[w, YY, 2:18, 7:8, :] = yrecv[0, :, k + 4:k + 5, :]
-        k = 8 * w
-        ST[w, XY, 2:18, 24:25, :] = yrecv[1, :, k:k + 1, :]
-        ST[w, YZ, 2:18, 24:25, :] = yrecv[1, :, k + 1:k + 2, :]
-        ST[w, YY, 2:18, 24:26, :] = yrecv[1, :, k + 2:k + 4, :]
+            y_copy(side).wait_recv()
+
+    for w in range(2):
+        k = 4 * w
+        ST[w, XY, 2:18, 6:8, :] = yrecv[0, 0:16, k:k + 2, :]
+        ST[w, YZ, 2:18, 6:8, :] = yrecv[0, 0:16, k + 2:k + 4, :]
+        ST[w, XY, 2:18, 24:25, :] = yrecv[1, 0:16, k:k + 1, :]
+        ST[w, YZ, 2:18, 24:25, :] = yrecv[1, 0:16, k + 1:k + 2, :]
+        ST[w, YY, 2:18, 24:26, :] = yrecv[1, 0:16, k + 2:k + 4, :]
+        for x in range(16):
+            k = 16 * w + x
+            ST[w, YY, 2 + x, 7:8, :] = yrecv[0, 16 + k // 8, k % 8:k % 8 + 1, :]
+
+    def accel_rows(i, carry):
+        accelerate(2 * i, 2)
+        return carry
+
+    lax.fori_loop(0, 8, accel_rows, 0)
+
+    for w in range(2):
+        k = 4 * w
+        for c, y, n in ((0, 15, 1), (1, 14, 2), (2, 15, 1)):
+            y2sb[:, k:k + n, :] = VE[w, c, 2:18, 8 + y:8 + y + n, :]
+            k += n
+        k = 4 * w
+        for c, n in ((0, 2), (1, 1), (2, 1)):
+            y2sa[0:16, k:k + n, :] = VE[w, c, 2:18, 8:8 + n, :]
+            k += n
+        for x in range(16):
+            k = 16 * w + x
+            y2sa[16 + k // 8, k % 8:k % 8 + 1, :] = VE[w, 2, 2 + x, 9:10, :]
+    for side in range(2):
+        @pl.when(exists_send_y[side])
+        def _():
+            y2_copy(side).start()
+    for side in range(2):
+        @pl.when(exists_recv_y[side])
+        def _():
+            rim_copy(side).wait_recv()
 
     items = (
         [(XX, 15), (XY, 14), (XY, 15), (XZ, 14), (XZ, 15), (YY, 15), (YZ, 15)],
         [(XX, 0), (XX, 1), (XY, 0), (XZ, 0), (YY, 0), (YY, 1), (YZ, 0), (YZ, 1)],
     )
-    where = {XX: (5, 1, 4, 2), XY: (0, 2, 0, 1), XZ: (6, 1, 6, 2), YY: (4, 1, 2, 2), YZ: (2, 2, 1, 1)}
     for side in range(2):
         for w in range(2):
             for i, (c, x) in enumerate(items[side]):
-                kb, nb, ka, na = where[c]
-                xe_send[side, w, 3 * i:3 * i + nb, :] = yrecv[0, x, 7 * w + kb:7 * w + kb + nb, :]
-                xe_send[side, w, 3 * i + nb:3 * i + 3, :] = yrecv[1, x, 8 * w + ka:8 * w + ka + na, :]
+                nb = 2 if c in (XY, YZ) else 1
+                if c in (XX, XZ):
+                    q, at = (0 if c == XX else 1), edges.index(x)
+                    before = rimrecv[0, at, 2 * w + q:2 * w + q + 1, :]
+                    after = rimrecv[1, at, 4 * w + 2 * q:4 * w + 2 * q + 2, :]
+                else:
+                    before = ST[w, c, 2 + x, 8 - nb:8, :]
+                    after = ST[w, c, 2 + x, 24:27 - nb, :]
+                xe_send[side, w, 3 * i:3 * i + nb, :] = before
+                xe_send[side, w, 3 * i + nb:3 * i + 3, :] = after
     send_x(2)
 
-    def accel_rows(i, carry):
-        accelerate(2 * i, 2)
-        return carry
-
-    lax.fori_loop(0, 8, accel_rows, 0)
-
-    for w in range(2):
-        k = 4 * w
-        for c, y, n in ((0, 15, 1), (1, 14, 2), (2, 15, 1)):
-            y2sb[:, k:k + n, :] = VE[w, c, 2:18, 8 + y:8 + y + n, :]
-            k += n
-        k = 5 * w
-        for c, y, n in ((0, 0, 2), (1, 0, 1), (2, 0, 2)):
-            y2sa[:, k:k + n, :] = VE[w, c, 2:18, 8 + y:8 + y + n, :]
-            k += n
-    for side in range(2):
-        @pl.when(exists_send_y[side])
-        def _():
-            y2_copy(side).start()
     relays = (low_relay, high_relay)
     for side in range(2):
         @pl.when(relays[side])
@@ -380,10 +404,13 @@
         for c, n in ((0, 1), (1, 2), (2, 1)):
             VE[w, c, 2:18, 8 - n:8, :] = y2rb[:, k:k + n, :]
             k += n
-        k = 5 * w
-        for c, n in ((0, 2), (1, 1), (2, 2)):
-            VE[w, c, 2:18, 24:24 + n, :] = y2ra[:, k:k + n, :]
+        k = 4 * w
+        for c, n in ((0, 2), (1, 1), (2, 1)):
+            VE[w, c, 2:18, 24:24 + n, :] = y2ra[0:16, k:k + n, :]
             k += n
+        for x in range(16):
+            k = 16 * w + x
+            VE[w, 2, 2 + x, 25:26, :] = y2ra[16 + k // 8, k % 8:k % 8 + 1, :]
 
     def finish(x0, n):
         lam = DT * LM[pl.ds(x0, n)]
@@ -435,9 +462,9 @@
         lower_part = sum(k * xe_recv[e, w, 3 * i:3 * i + nb, :] for i, k in terms)
         upper_part = sum(k * xe_recv[e, w, 3 * i + nb:3 * i + 3, :] for i, k in terms)
         r = x if e == 0 else x - 14
-        VE[w, c, 2 + x, 8 - nb:8, :] = VE[w, c, 2 + x, 8 - nb:8, :] + byrecv[0, e, r, 8 - nb:8, :] * lower_part
+        VE[w, c, 2 + x, 8 - nb:8, :] = VE[w, c, 2 + x, 8 - nb:8, :] + rimrecv[0, 4 + 2 * e + r, 8 - nb:8, :] * lower_part
         na = 3 - nb
-        VE[w, c, 2 + x, 24:24 + na, :] = VE[w, c, 2 + x, 24:24 + na, :] + byrecv[1, e, r, 0:na, :] * upper_part
+        VE[w, c, 2 + x, 24:24 + na, :] = VE[w, c, 2 + x, 24:24 + na, :] + rimrecv[1, 4 + 2 * e + r, 0:na, :] * upper_part
 
     def rim(w, c, x, e, scale, i, forward):
         def f(k):
@@ -537,8 +564,8 @@
     for side in range(2):
         @pl.when(exists_send_y[side])
         def _():
-            for c in y_copies(side):
-                c.wait_send()
+            y_copy(side).wait_send()
+            rim_copy(side).wait_send()
             y2_copy(side).wait_send()
 
         @pl.when(near[side])
@@ -590,8 +617,8 @@
             buf(20, 32, 128), buf(16, 16, 128), buf(16, 16, 128), buf(16, 16, 128),
             buf(1, 256, dtype=jnp.int32), buf(1, 256),
             pltpu.SMEM((2,), F32),
-            buf(2, 16, 16, 128), buf(2, 16, 16, 128), buf(2, 2, 2, 8, 128), buf(2, 2, 2, 8, 128),
-            buf(16, 8, 128), buf(16, 16, 128), buf(16, 8, 128), buf(16, 16, 128),
+            buf(2, 20, 8, 128), buf(2, 20, 8, 128), buf(2, 8, 8, 128), buf(2, 8, 8, 128),
+            buf(16, 8, 128), buf(20, 8, 128), buf(16, 8, 128), buf(20, 8, 128),
             buf(2, 10, 16, 128), buf(2, 10, 16, 128), buf(2, 2, 24, 128),
             buf(2, 10, 16, 128), buf(2, 10, 16, 128), buf(2, 2, 24, 128),
             buf(2, 16, 128), buf(3, 16, 128), buf(3, 16, 16, 128), buf(3, 16, 16, 128),

time: 36.9 us -> 34.7 us (0.940)
  the two profiles are of different devices: /device:TPU:127 before, /device:TPU:57 now
where the time goes in v3:
time: 34.7 us; the launch traced here: 34.6 us
  Pallas kernels  32.1 us (93%)
  between operations  1.93 us (6%)
  other arithmetic  0.59 us (2%)
    pallas_call x1, Pallas kernels, body(): pl.pallas_call(step_kernel, out_shape=(pltpu.VMEM(fields, F32), pltpu.VME...  30.5 us
    pallas_call x1, Pallas kernels, body(): pl.pallas_call(store_kernel, out_shape=tuple((jax.ShapeDtypeStruct(shape,...  1.55 us

profile of v3, /device:TPU:57, one launch (start us, length us, event | category | flops | bytes accessed | tf_op | source)
XLA Modules:
  0.0 34.6 jit_solution(4321793081747421876)
XLA Ops:
  1.9 0.6 %pad_maximum_fusion.source_h = f32[2]{0:T(128)} fusion(f32[1]{0:T(128)S(6)} %copy.13, f32[1]{0:T(128)S(6)} %convert_element_type.3), kind=kLoop, calls=%fused_computation | loop fusion | flops 2 | bytes 16 | tf_op jit(solution)/shard_map/concatenate | solution.py:605
  2.5 30.5 %step.1 = (f32[9,16,16,128]{3,2,1,0:T(8,128)S(1)}, f32[9,16,16,128]{3,2,1,0:T(8,128)S(1)}, f32[3,16,16,128]{3,2,1,0:T(8,128)S(1)}) custom-call(f32[1,9,16,16,128]{4,3,2,1,0:T(8,128)} %fwd.1, f32[1,9,16,16,128]{4,3,2,1,0:T(8,128)} %adj.1, f32[16,16,128]{2,1,0:T(8,128)} %lam_h.1, f32[16,16,128]{2,1,0:T(8,128)} %mu_h.1, f32[16,16,128]{2,1,0:T(8,128)} %den_h.1, ...), custom_call_target="tpu_custom_call" | custom-call | tf_op jit(solution)/shard_map/step/pallas_call | solution.py:610
  33.0 1.6 %store.1 = (f32[9,16,16,128]{3,2,1,0:T(8,128)}, f32[9,16,16,128]{3,2,1,0:T(8,128)}, f32[3,16,16,128]{3,2,1,0:T(8,128)}) custom-call(f32[9,16,16,128]{3,2,1,0:T(8,128)S(1)} %get-tuple-element.9.f, f32[9,16,16,128]{3,2,1,0:T(8,128)S(1)} %get-tuple-element.10.a, f32[3,16,16,128]{3,2,1,0:T(8,128)S(1)} %get-tuple-element.11.g), custom_call_target="tpu_custom_call" | custom-call | tf_op jit(solution)/shard_map/store/pallas_call | solution.py:633

commit v4 on v3

--- a/solution.py
+++ b/solution.py
@@ -16,9 +16,9 @@
 
 
 def step_kernel(
-    fwd, adj, lam_h, mu_h, den_h, source_h, rcell_h, ramp_h,
+    fwd, adj, lam_h, mu_h, den_h, scell_h, samp_h, rcell_h, ramp_h,
     f_out, a_out, g_out,
-    ST, VE, VO, AC, BU, LM, MU, ADD, rcell, ramp, source,
+    ST, VE, VO, AC, BU, LM, MU, ADD, rcell, ramp, scell, samp,
     ysend, yrecv, rimsend, rimrecv, y2sb, y2sa, y2rb, y2ra,
     xs_send, xv_send, xe_send, xs_recv, xv_recv, xe_recv, rel_s, rel_v, GL, GR,
     in_sem, y_ss, y_rs, x_ss, x_rs, rel_ss, rel_rs, g_ss, g_rs,
@@ -54,7 +54,8 @@
         (adj.at[0, pl.ds(3, 6)], ST.at[1, :, pl.ds(2, 16), pl.ds(8, 16)]),
         (rcell_h, rcell),
         (ramp_h, ramp),
-        (source_h, source),
+        (scell_h, scell),
+        (samp_h, samp),
         (den_h, BU.at[pl.ds(2, 16), pl.ds(8, 16)]),
         (fwd.at[0, pl.ds(0, 3)], VO.at[0]),
         (adj.at[0, pl.ds(0, 3)], VO.at[1]),
@@ -90,7 +91,7 @@
                 ST[w, c, 2:18, lo:lo + 8, :] = jnp.zeros((16, 8, 128), F32)
     rimsend[0, 0:4] = jnp.zeros((4, 8, 128), F32)
 
-    for c in copies[2:5]:
+    for c in copies[2:6]:
         c.wait()
 
     def place(cell):
@@ -119,7 +120,7 @@
         gx = lax.broadcasted_iota(jnp.int32, shape, 0) + (2 * i + tx * 16)
         gy = lax.broadcasted_iota(jnp.int32, shape, 1) + ty * 16
         cell = gx * 65536 + gy * 128 + lax.broadcasted_iota(jnp.int32, shape, 2)
-        src = jnp.where(cell.astype(F32) == source[0], source[1], 0.0)
+        src = jnp.where(cell == scell[0], samp[0], 0.0)
         rows = pl.ds(2 + 2 * i, 2)
         for c in range(3):
             ST[0, c, rows, 8:24, :] = ST[0, c, rows, 8:24, :] + src
@@ -127,7 +128,7 @@
         return carry
 
     lax.fori_loop(0, 8, inject_rows, 0)
-    copies[5].wait()
+    copies[6].wait()
     BU[2:18, 8:24, :] = DT / BU[2:18, 8:24, :]
 
     for w in range(2):
@@ -214,7 +215,7 @@
                     AC[c, pl.ds(x0, n)] = step
                 VE[w, c, pl.ds(2 + x0, n), 8:24, :] = VO[w, c, pl.ds(x0, n)] + step
 
-    for c in copies[6:]:
+    for c in copies[7:]:
         c.wait()
     accelerate(0, 2)
     accelerate(14, 2)
@@ -602,34 +603,32 @@
     vmem = pl.BlockSpec(memory_space=pltpu.VMEM)
     dma = pltpu.SemaphoreType.DMA
 
-    source = jnp.concatenate([scell.astype(F32), samp])
-
     def buf(*shape, dtype=F32):
         return pltpu.VMEM(shape, dtype)
 
     f, a, g = pl.pallas_call(
         step_kernel,
         out_shape=(pltpu.VMEM(fields, F32), pltpu.VMEM(fields, F32), pltpu.VMEM(grads, F32)),
-        in_specs=[hbm] * 8,
+        in_specs=[hbm] * 9,
         out_specs=(vmem, vmem, vmem),
         scratch_shapes=[
             buf(2, 6, 20, 32, 128), buf(2, 3, 20, 32, 128), buf(2, 3, 16, 16, 128), buf(3, 16, 16, 128),
             buf(20, 32, 128), buf(16, 16, 128), buf(16, 16, 128), buf(16, 16, 128),
             buf(1, 256, dtype=jnp.int32), buf(1, 256),
-            pltpu.SMEM((2,), F32),
+            pltpu.SMEM((1,), jnp.int32), pltpu.SMEM((1,), F32),
             buf(2, 20, 8, 128), buf(2, 20, 8, 128), buf(2, 8, 8, 128), buf(2, 8, 8, 128),
             buf(16, 8, 128), buf(20, 8, 128), buf(16, 8, 128), buf(20, 8, 128),
             buf(2, 10, 16, 128), buf(2, 10, 16, 128), buf(2, 2, 24, 128),
             buf(2, 10, 16, 128), buf(2, 10, 16, 128), buf(2, 2, 24, 128),
             buf(2, 16, 128), buf(3, 16, 128), buf(3, 16, 16, 128), buf(3, 16, 16, 128),
-            dma((10,)), dma((2, 4)), dma((2, 4)), dma((2, 3, 4)), dma((2, 3, 4)),
+            dma((11,)), dma((2, 4)), dma((2, 4)), dma((2, 3, 4)), dma((2, 3, 4)),
             dma((2,)), dma((2,)), dma((3,)), dma((3,)),
         ],
         compiler_params=pltpu.CompilerParams(
             collective_id=1, has_side_effects=True, vmem_limit_bytes=56 * 1024 * 1024
         ),
         name="step",
-    )(fwd, adj, lam, mu, den, source, rcell, ramp)
+    )(fwd, adj, lam, mu, den, scell, samp, rcell, ramp)
     f, a, g = pl.pallas_call(
         store_kernel,
         out_shape=tuple(jax.ShapeDtypeStruct(shape, F32) for shape in (fields, fields, grads)),

time: 34.7 us -> 34.2 us (0.986)
  other arithmetic: 0.59 us -> 0 us
    concatenate x1 -> x0, other arithmetic: 0.59 us -> none  [body(): source = jnp.concatenate([scell.astype(F32), samp])]
where the time goes in v4:
time: 34.2 us; the launch traced here: 34 us
  Pallas kernels  32.1 us (94%)
  between operations  1.93 us (6%)
    pallas_call x1, Pallas kernels, body(): pl.pallas_call(step_kernel, out_shape=(pltpu.VMEM(fields, F32), pltpu.VME...  30.5 us
    pallas_call x1, Pallas kernels, body(): pl.pallas_call(store_kernel, out_shape=tuple((jax.ShapeDtypeStruct(shape,...  1.55 us

profile of v4, /device:TPU:57, one launch (start us, length us, event | category | flops | bytes accessed | tf_op | source)
XLA Modules:
  0.0 34.0 jit_solution(1923237393762136694)
XLA Ops:
  1.9 30.5 %step.1 = (f32[9,16,16,128]{3,2,1,0:T(8,128)S(1)}, f32[9,16,16,128]{3,2,1,0:T(8,128)S(1)}, f32[3,16,16,128]{3,2,1,0:T(8,128)S(1)}) custom-call(f32[1,9,16,16,128]{4,3,2,1,0:T(8,128)} %fwd.1, f32[1,9,16,16,128]{4,3,2,1,0:T(8,128)} %adj.1, f32[16,16,128]{2,1,0:T(8,128)} %lam_h.1, f32[16,16,128]{2,1,0:T(8,128)} %mu_h.1, f32[16,16,128]{2,1,0:T(8,128)} %den_h.1, ...), custom_call_target="tpu_custom_call" | custom-call | tf_op jit(solution)/shard_map/step/pallas_call | solution.py:609
  32.5 1.6 %store.1 = (f32[9,16,16,128]{3,2,1,0:T(8,128)}, f32[9,16,16,128]{3,2,1,0:T(8,128)}, f32[3,16,16,128]{3,2,1,0:T(8,128)}) custom-call(f32[9,16,16,128]{3,2,1,0:T(8,128)S(1)} %get-tuple-element.9.f, f32[9,16,16,128]{3,2,1,0:T(8,128)S(1)} %get-tuple-element.10.a, f32[3,16,16,128]{3,2,1,0:T(8,128)S(1)} %get-tuple-element.11.g), custom_call_target="tpu_custom_call" | custom-call | tf_op jit(solution)/shard_map/store/pallas_call | solution.py:632

commit v5 on v4

--- a/solution.py
+++ b/solution.py
@@ -345,7 +345,7 @@
         accelerate(2 * i, 2)
         return carry
 
-    lax.fori_loop(0, 8, accel_rows, 0)
+    lax.fori_loop(0, 8, accel_rows, 0, unroll=True)
 
     for w in range(2):
         k = 4 * w
@@ -455,7 +455,7 @@
         finish(2 * i, 2)
         return carry
 
-    lax.fori_loop(2, 6, finish_rows, 0)
+    lax.fori_loop(2, 6, finish_rows, 0, unroll=True)
     g_copy(0).start()
 
     def correct(w, c, x, e, terms):
@@ -542,7 +542,7 @@
             accelerate(14, 2)
             first = 6
 
-        lax.fori_loop(first, first + 2, finish_rows, 0)
+        lax.fori_loop(first, first + 2, finish_rows, 0, unroll=True)
         g_copy(1 + side).start()
 
     @pl.when(jnp.logical_not(is4))

time: 34.2 us -> 33.3 us (0.974)
  Pallas kernels: 32.1 us -> 31.2 us
    pallas_call x1, Pallas kernels: 30.5 us -> 29.7 us  [body(): pl.pallas_call(step_kernel, out_shape=(pltpu.VMEM(fields, F32), pltpu.VME...]
where the time goes in v5:
time: 33.3 us; the launch traced here: 33.2 us
  Pallas kernels  31.2 us (94%)
  between operations  1.93 us (6%)
    pallas_call x1, Pallas kernels, body(): pl.pallas_call(step_kernel, out_shape=(pltpu.VMEM(fields, F32), pltpu.VME...  29.7 us
    pallas_call x1, Pallas kernels, body(): pl.pallas_call(store_kernel, out_shape=tuple((jax.ShapeDtypeStruct(shape,...  1.55 us

profile of v5, /device:TPU:57, one launch (start us, length us, event | category | flops | bytes accessed | tf_op | source)
XLA Modules:
  0.0 33.2 jit_solution(714894484630854980)
XLA Ops:
  1.9 29.7 %step.1 = (f32[9,16,16,128]{3,2,1,0:T(8,128)S(1)}, f32[9,16,16,128]{3,2,1,0:T(8,128)S(1)}, f32[3,16,16,128]{3,2,1,0:T(8,128)S(1)}) custom-call(f32[1,9,16,16,128]{4,3,2,1,0:T(8,128)} %fwd.1, f32[1,9,16,16,128]{4,3,2,1,0:T(8,128)} %adj.1, f32[16,16,128]{2,1,0:T(8,128)} %lam_h.1, f32[16,16,128]{2,1,0:T(8,128)} %mu_h.1, f32[16,16,128]{2,1,0:T(8,128)} %den_h.1, ...), custom_call_target="tpu_custom_call" | custom-call | tf_op jit(solution)/shard_map/step/pallas_call | solution.py:609
  31.6 1.6 %store.1 = (f32[9,16,16,128]{3,2,1,0:T(8,128)}, f32[9,16,16,128]{3,2,1,0:T(8,128)}, f32[3,16,16,128]{3,2,1,0:T(8,128)}) custom-call(f32[9,16,16,128]{3,2,1,0:T(8,128)S(1)} %get-tuple-element.9.f, f32[9,16,16,128]{3,2,1,0:T(8,128)S(1)} %get-tuple-element.10.a, f32[3,16,16,128]{3,2,1,0:T(8,128)S(1)} %get-tuple-element.11.g), custom_call_target="tpu_custom_call" | custom-call | tf_op jit(solution)/shard_map/store/pallas_call | solution.py:632
